TPU v7x, 32 devices: a whole 2x2x4 slice. The times are simulated.
32 devices in a mesh: clu: 4 (over z), ang: 8 (over y, x, core).
Axes of the slice: x: 2, y: 2, z: 4, core: 2. Of those that a mesh axis runs over, the one named last changes fastest.
Arguments:
- patterns7: bfloat16 [8192, 2, 64, 128], P(('clu', 'ang')), may hold values from -6 to 6
- polar_up7: bfloat16 [128, 64], replicated, may hold values from -0.25 to 0.25
- azimuth_up7: bfloat16 [128, 256], replicated, may hold values from -0.5 to 0.5
- polar_up6: bfloat16 [256, 128], replicated, may hold values from -0.1875 to 0.1875
- azimuth_up6: bfloat16 [256, 512], replicated, may hold values from -0.375 to 0.375
- polar_first: int32 [512], replicated, may hold values from 0 to 252, as said below
- polar_weights: bfloat16 [512, 4], replicated, may hold values from -1 to 1
- azimuth_first: int32 [1024], replicated, may hold values from 0 to 511, as said below
- azimuth_weights: bfloat16 [1024, 4], replicated, may hold values from -3 to 3
- transfer5: bfloat16 [316, 2, 256, 512], P(None, None, 'ang', 'clu'), may hold values from -1.5 to 1.5
- sources5: int32 [128, 16], replicated, may hold values from -1 to 127, as said below
- offsets5: int32 [128, 16], replicated, may hold values from -1 to 315, as said below
- transfer4: bfloat16 [316, 2, 512, 1024], P(None, None, 'ang', 'clu'), may hold values from -1.5 to 1.5
- sources4: int32 [16, 16], replicated, may hold values from -1 to 15, as said below
- offsets4: int32 [16, 16], replicated, may hold values from -1 to 315, as said below
Outputs:
- translated5: bfloat16 [128, 2, 256, 512], P(None, None, 'ang', 'clu')
- translated4: bfloat16 [16, 2, 512, 1024], P(None, None, 'ang', 'clu')
Inputs may be any that keep to these rules, and one draw needn't show every extreme that they name: The theta stencil of target row r reads source rows polar_first[r] to polar_first[r] + 3, all within floor(r / 2) - 3 to floor(r / 2) + 3. The phi stencil of target column c reads source columns (azimuth_first[c] + k) mod 512, k = 0 to 3, all within floor(c / 2) - 3 to floor(c / 2) + 3 modulo 512. `sources5`: row t lists source clusters of target t: live entries first, then -1; never t itself; at least one live entry. `offsets5`: displacement id of each slot; -1 exactly where sources5 is -1. `sources4`: row t lists source clusters of target t: live entries first, then -1; never t itself; at least one live entry. `offsets4`: displacement id of each slot; -1 exactly where sources4 is -1.
All inputs are finite; a program needn't handle non-finite values.
Results may differ from a plain program's by a relative error of at most 0.015.
Values may be sent and summed in bfloat16 or wider, within the bound.
A program may use at most 192 MiB of HBM per device.

v0:
```python
import math

import jax
import jax.numpy as jnp
from jax import lax
from jax.sharding import PartitionSpec as P


def extended_2(block, sides, width, periodic):
    for axis, dim in sides:
        count = lax.axis_size(axis)
        forward = [(i, i + 1) for i in range(count - 1)]
        if periodic:
            forward.append((count - 1, 0))
        backward = [(target, source) for source, target in forward]
        low = lax.ppermute(
            lax.slice_in_dim(block, block.shape[dim] - width, None, axis=dim), axis, forward
        )
        high = lax.ppermute(lax.slice_in_dim(block, 0, width, axis=dim), axis, backward)
        block = jnp.concatenate([low, block, high], axis=dim)
    return block


def octant_signs():
    octant = jnp.arange(8, dtype=jnp.int32)
    sign_first = (2 * (octant % 2) - 1).astype(jnp.float32)
    sign_second = (2 * (octant // 2 % 2) - 1).astype(jnp.float32)
    sign_third = (2 * (octant // 4) - 1).astype(jnp.float32)
    return (sign_first, sign_second, sign_third)


def phase_tables(polar_index, azimuth_index, polar_count, azimuth_count):
    polar_angle = (polar_index + 0.5) * (math.pi / polar_count)
    azimuth_angle = azimuth_index * (2.0 * math.pi / azimuth_count)
    direction_x = jnp.sin(polar_angle)[:, None] * jnp.cos(azimuth_angle)[None, :]
    direction_y = jnp.sin(polar_angle)[:, None] * jnp.sin(azimuth_angle)[None, :]
    direction_z = jnp.cos(polar_angle)[:, None] * jnp.ones_like(azimuth_angle)[None, :]
    sign_first, sign_second, sign_third = octant_signs()
    phase_angle = (
        polar_count
        / 8.0
        * (
            sign_first[:, None, None] * direction_x
            + sign_second[:, None, None] * direction_y
            + sign_third[:, None, None] * direction_z
        )
    )
    return (jnp.cos(phase_angle), jnp.sin(phase_angle))


def shift_sum(child_terms, cosine, sine):
    real_part = jnp.sum(child_terms[:, :, 0] * cosine - child_terms[:, :, 1] * sine, axis=1)
    imag_part = jnp.sum(child_terms[:, :, 0] * sine + child_terms[:, :, 1] * cosine, axis=1)
    return jnp.stack([real_part, imag_part], axis=1).astype(jnp.bfloat16)


def stencil_matrix(tap_index, weights, column_count):
    matches = (
        tap_index[:, :, None] == jnp.arange(column_count, dtype=jnp.int32)[None, None, :]
    ).astype(jnp.float32)
    return jnp.sum(weights.astype(jnp.float32)[:, :, None] * matches, axis=1)


def parent_block(children, polar_matrix, azimuth_matrix, cosine, sine):
    parents = children.shape[0] // 8
    grouped = children.reshape(parents, 8, 2, children.shape[2], children.shape[3])
    halfway = jnp.einsum(
        "ut,pkcts->pkcus", polar_matrix, grouped, preferred_element_type=jnp.float32
    ).astype(jnp.bfloat16)
    child_terms = jnp.einsum(
        "pkcus,sv->pkcuv", halfway, azimuth_matrix, preferred_element_type=jnp.float32
    )
    return shift_sum(child_terms, cosine, sine)


def aggregate(children, polar_matrix, azimuth_matrix, cosine, sine, block_parents):
    parent_total = children.shape[0] // 8
    group_size = math.gcd(parent_total, block_parents)
    blocks = children.reshape(
        parent_total // group_size, group_size * 8, 2, children.shape[2], children.shape[3]
    )

    def one_block(block_piece):
        return parent_block(block_piece, polar_matrix, azimuth_matrix, cosine, sine)

    merged = lax.map(one_block, blocks)
    return merged.reshape(parent_total, 2, polar_matrix.shape[0], azimuth_matrix.shape[1])


def translate(patterns, transfer_table, sources, displacements):
    targets = patterns.shape[0]
    flat_patterns = patterns.reshape(targets, 2, -1)
    flat_table = transfer_table.reshape(transfer_table.shape[0], 2, -1)
    samples = flat_patterns.shape[2]
    slots = sources.shape[1]

    def add_slot(slot, totals):
        real_total, imag_total = totals
        source_col = lax.dynamic_index_in_dim(sources, slot, 1, keepdims=False)
        offset_col = lax.dynamic_index_in_dim(displacements, slot, 1, keepdims=False)
        live_slot = (source_col >= 0)[:, None]
        picked = jnp.take(flat_patterns, jnp.maximum(source_col, 0), axis=0)
        factor = jnp.take(flat_table, jnp.maximum(offset_col, 0), axis=0)
        factor_real = jnp.where(live_slot, factor[:, 0].astype(jnp.float32), 0.0)
        factor_imag = jnp.where(live_slot, factor[:, 1].astype(jnp.float32), 0.0)
        picked_real = picked[:, 0].astype(jnp.float32)
        picked_imag = picked[:, 1].astype(jnp.float32)
        real_total = real_total + factor_real * picked_real - factor_imag * picked_imag
        imag_total = imag_total + factor_real * picked_imag + factor_imag * picked_real
        return (real_total, imag_total)

    empty = jnp.zeros((targets, samples), jnp.float32)
    real_total, imag_total = lax.fori_loop(0, slots, add_slot, (empty, empty))
    return jnp.stack([real_total, imag_total], axis=1).astype(jnp.bfloat16).reshape(patterns.shape)


def band_windows(level5, band_count, block_count):
    local_count = level5.shape[0]
    rows_five = level5.shape[2]
    cols_five = level5.shape[3]
    source_rows = rows_five // band_count
    source_cols = cols_five // block_count
    spread = level5.reshape(local_count, 2, band_count, source_rows, block_count, source_cols)
    return spread.transpose(0, 4, 2, 1, 3, 5)


def shards(
    patterns7,
    polar_up7,
    azimuth_up7,
    polar_up6,
    azimuth_up6,
    polar_first,
    polar_weights,
    azimuth_first,
    azimuth_weights,
    transfer5,
    sources5,
    offsets5,
    transfer4,
    sources4,
    offsets4,
):
    rows_six = polar_up7.shape[0]
    cols_six = azimuth_up7.shape[1]
    cosine6, sine6 = phase_tables(
        jnp.arange(rows_six, dtype=jnp.float32),
        jnp.arange(cols_six, dtype=jnp.float32),
        rows_six,
        cols_six,
    )
    level6 = aggregate(patterns7, polar_up7, azimuth_up7, cosine6, sine6, 8)
    rows_five = polar_up6.shape[0]
    cols_five = azimuth_up6.shape[1]
    cosine5, sine5 = phase_tables(
        jnp.arange(rows_five, dtype=jnp.float32),
        jnp.arange(cols_five, dtype=jnp.float32),
        rows_five,
        cols_five,
    )
    level5 = aggregate(level6, polar_up6, azimuth_up6, cosine5, sine5, 8)
    band_count = lax.axis_size("ang")
    block_count = lax.axis_size("clu")
    source_rows = rows_five // band_count
    source_cols = cols_five // block_count
    local_count = level5.shape[0]
    margin = 0
    window_rows = source_rows + 2 * margin
    window_cols = source_cols + 2 * margin
    spread = band_windows(level5, band_count, block_count)
    flat_spread = spread.reshape(local_count, block_count * band_count, 2, window_rows, window_cols)
    arrived = lax.all_to_all(flat_spread, ("clu", "ang"), split_axis=1, concat_axis=0, tiled=True)
    arrived = arrived.reshape(local_count * block_count * band_count, 2, window_rows, window_cols)
    translated5 = translate(arrived, transfer5, sources5, offsets5)
    rows_four = polar_first.shape[0]
    cols_four = azimuth_first.shape[0]
    band_rows = rows_four // band_count
    block_cols = cols_four // block_count
    band_index = lax.axis_index("ang")
    column_block = lax.axis_index("clu")
    four_taps = jnp.arange(4, dtype=jnp.int32)[None, :]
    polar_local = (
        lax.dynamic_slice_in_dim(polar_first, band_index * band_rows, band_rows, 0)
        - band_index * source_rows
        + 3
    )
    polar_local_weights = lax.dynamic_slice_in_dim(
        polar_weights, band_index * band_rows, band_rows, 0
    )
    polar_matrix = stencil_matrix(
        polar_local[:, None] + four_taps, polar_local_weights, source_rows + 6
    ).astype(jnp.bfloat16)
    azimuth_local = (
        lax.dynamic_slice_in_dim(azimuth_first, column_block * block_cols, block_cols, 0)
        - column_block * source_cols
        + 3
    ) % cols_five
    azimuth_local_weights = lax.dynamic_slice_in_dim(
        azimuth_weights, column_block * block_cols, block_cols, 0
    )
    azimuth_matrix = stencil_matrix(
        azimuth_local[:, None] + four_taps, azimuth_local_weights, source_cols + 6
    ).T.astype(jnp.bfloat16)
    extended = extended_2(arrived, (("ang", 2),), 3, False)
    halfway = jnp.einsum(
        "uq,ncqf->ncuf", polar_matrix, extended, preferred_element_type=jnp.float32
    ).astype(jnp.bfloat16)
    widened = extended_2(halfway, (("clu", 3),), 3, True)
    child_terms = jnp.einsum(
        "ncuq,qv->ncuv", widened, azimuth_matrix, preferred_element_type=jnp.float32
    )
    polar_index = (jnp.arange(band_rows, dtype=jnp.int32) + band_index * band_rows).astype(
        jnp.float32
    )
    azimuth_index = (jnp.arange(block_cols, dtype=jnp.int32) + column_block * block_cols).astype(
        jnp.float32
    )
    cosine4, sine4 = phase_tables(polar_index, azimuth_index, rows_four, cols_four)
    parent_count = child_terms.shape[0] // 8
    level4 = shift_sum(
        child_terms.reshape(parent_count, 8, 2, band_rows, block_cols), cosine4, sine4
    )
    translated4 = translate(level4, transfer4, sources4, offsets4)
    return (translated5, translated4)


def solution(mesh):
    in_specs = (
        P(("clu", "ang"), None, None, None),
        P(),
        P(),
        P(),
        P(),
        P(),
        P(),
        P(),
        P(),
        P(None, None, "ang", "clu"),
        P(),
        P(),
        P(None, None, "ang", "clu"),
        P(),
        P(),
    )
    out_specs = (P(None, None, "ang", "clu"), P(None, None, "ang", "clu"))
    return jax.shard_map(shards, mesh=mesh, in_specs=in_specs, out_specs=out_specs, check_vma=False)
```

profile of v0, /device:TPU:4, one launch (start us, length us, event | category | flops | bytes accessed | tf_op | source)
XLA Modules:
  0.0 1372.3 jit_solution(10405957768337510713)
XLA Ops:
  2.8 97.2 %while.51 = (s32[]{:T(128)}, bf16[4,8,2,128,256]{4,3,2,1,0:T(8,128)(2,1)}, bf16[4,64,2,64,128]{4,3,2,1,0:T(8,128)(2,1)}, bf16[128,64]{0,1:T(8,128)(2,1)}, bf16[1...) while((s32[]{:T(128)}, ...), condition=%wide.region_3.4_spmd.clone.clone.clone, body=%wide.region_0.3_spmd.clone.clone.clone.sunk | while | flops 1364197376 | bytes 48650508 | solution.py:86
  100.9 17.8 %fusion.35 = (f32[8,256,512]{2,1,0:T(8,128)}, f32[8,256,512]{2,1,0:T(8,128)}) fusion(f32[256]{0:T(256)} %fusion.55, f32[8]{0:T(128)S(1)} %get-tuple-element.932, f32[256,512]{1,0:T(8,128)S(1)} %get-tuple-element.624, f32[8]{0:T(128)S(1)} %get-tuple-element.934, f32[256,512]{1,0:T(8,128)S(1)} %get-tuple-element.623, f32[8]{0:T(128)S(1)} %get-tuple-element.933), kind=kLoop, calls=%fused_computation.92 | loop fusion | flops 6291456 | bytes 9438304 | tf_op jit(solution)/shard_map/cos | solution.py:48
  118.8 16.1 %fusion.24 = f32[4,8,2,256,512]{4,3,2,1,0:T(8,128)} fusion(bf16[4,8,2,128,256]{4,3,2,1,0:T(8,128)(2,1)} %get-tuple-element.316, bf16[256,512]{1,0:T(8,128)(2,1)S(1)} %copy-done, bf16[256,128]{1,0:T(8,128)(2,1)S(1)} %copy-done.8), kind=kOutput, calls=%fused_computation.80 | convolution fusion | flops 5372903424 | bytes 38076416 | tf_op jit(solution)/shard_map/while/body/eval_jaxpr/pkcus,sv->pkcuv/dot_general | solution.py:70
  134.8 15.1 %subtract_reduce_fusion.1 = (bf16[4,256,512]{2,1,0:T(8,128)(2,1)S(1)}, bf16[4,256,512]{2,1,0:T(8,128)(2,1)S(1)}) fusion(f32[4,8,2,256,512]{4,3,2,1,0:T(8,128)} %fusion.24, f32[8,256,512]{2,1,0:T(8,128)} %get-tuple-element.620, f32[8,256,512]{2,1,0:T(8,128)} %get-tuple-element.619), kind=kLoop, calls=%fused_computation.76 | loop fusion | flops 32505856 | bytes 44040192 | tf_op jit(solution)/shard_map/while/body/eval_jaxpr/reduce_sum | solution.py:52
  160.0 42.0 %reshape.468 = bf16[316,2,16384]{2,1,0:T(2,128)(2,1)} reshape(bf16[316,2,64,256]{3,2,1,0:T(8,128)(2,1)} %param.33) | data formatting | bytes 41418752 | tf_op jit(solution)/shard_map/reshape | solution.py:93
  202.2 10.7 reshape.465
  228.3 692.2 %while.49 = (s32[]{:T(128)}, f32[128,4096]{1,0:T(8,128)}, f32[128,4096]{1,0:T(8,128)}, s32[128,16]{0,1:T(8,128)}, s32[128,16]{0,1:T(8,128)}, /*index=5*/bf16[316...) while((s32[]{:T(128)}, f32[128,4096]{1,0:T(8,128)}, ...), condition=%wide.region_7.8_spmd.clone, body=%wide.region_6.7_spmd.clone.sunk | while | flops 10488707 | bytes 35665772 | solution.py:113
  313.3 10.4 fusion.91
  355.9 10.4 fusion.91
  398.6 10.4 fusion.91
  441.2 10.4 fusion.91
  483.9 10.4 fusion.91
  526.5 10.4 fusion.91
  569.2 10.4 fusion.91
  611.8 10.4 fusion.91
  654.4 10.4 fusion.91
  697.1 10.4 fusion.91
  739.7 10.4 fusion.91
  782.3 10.4 fusion.91
  824.8 10.4 fusion.91
  867.3 10.4 fusion.91
  963.9 10.8 pad_maximum_fusion
  974.7 12.8 fusion.29
  997.3 370.7 %while.50 = (s32[]{:T(128)}, f32[16,16384]{1,0:T(8,128)}, f32[16,16384]{1,0:T(8,128)}, s32[16,16]{0,1:T(8,128)S(1)}, s32[16,16]{0,1:T(8,128)S(1)}, /*index=5*/bf...) while((s32[]{:T(128)}, f32[16,16384]{1,0:T(8,128)}, ...), condition=%wide.region_13.14_spmd.clone, body=%wide.region_12.13_spmd.clone.sunk | while | flops 5245043 | bytes 17834832 | solution.py:113
  (512 shorter events, 1086.0 us)
Async XLA Ops:
  0.6 118.1 %copy-start = (bf16[256,512]{1,0:T(8,128)(2,1)S(1)}, bf16[256,512]{1,0:T(8,128)(2,1)}, u32[]{:S(2)}) copy-start(bf16[256,512]{1,0:T(8,128)(2,1)} %param.25) | copy-start | bytes 786436
  42.8 8.6 copy-start.15
  42.8 8.6 copy-start.19
  42.8 8.6 copy-start.23
  91.4 8.6 copy-start.7
  91.4 8.6 copy-start.11
  91.4 8.6 copy-start.15
  91.4 8.6 copy-start.19
  91.4 8.6 copy-start.23
  100.0 18.7 %copy-start.12 = (f32[8]{0:T(128)}, f32[8]{0:T(128)S(1)}, u32[]{:S(2)}) copy-start(f32[8]{0:T(128)S(1)} %get-tuple-element.932) | copy-start | bytes 100
  100.1 18.7 %copy-start.16 = (f32[8]{0:T(128)}, f32[8]{0:T(128)S(1)}, u32[]{:S(2)}) copy-start(f32[8]{0:T(128)S(1)} %get-tuple-element.933) | copy-start | bytes 100
  100.1 18.7 %copy-start.20 = (f32[8]{0:T(128)}, f32[8]{0:T(128)S(1)}, u32[]{:S(2)}) copy-start(f32[8]{0:T(128)S(1)} %get-tuple-element.934) | copy-start | bytes 100
  100.9 17.8 %copy-start.8 = (bf16[256,128]{1,0:T(8,128)(2,1)S(1)}, bf16[256,128]{1,0:T(8,128)(2,1)}, u32[]{:S(2)}) copy-start(bf16[256,128]{1,0:T(8,128)(2,1)} %param.24) | copy-start | bytes 196612
  153.9 64.7 %all-to-all-start = ((bf16[4,32,2,32,128]{4,3,2,0,1:T(8,128)(2,1)}), bf16[4,32,2,32,128]{4,3,2,0,1:T(8,128)(2,1)S(1)}, u32[]{:S(2)}, u32[]{:S(2)}) async-start(bf16[4,32,2,32,128]{4,3,2,0,1:T(8,128)(2,1)} %bitcast.246), calls=%async_computation | async-start | bytes 4194304 | tf_op jit(solution)/shard_map/all_to_all | solution.py:172
  160.0 42.0 %copy-start.24 = (s32[16,16]{1,0:T(8,128)S(1)}, s32[16,16]{1,0:T(8,128)}, u32[]{:S(2)}) copy-start(s32[16,16]{1,0:T(8,128)} %param.34) | copy-start | bytes 3076
  160.0 42.1 %copy-start.25 = (s32[16,16]{1,0:T(8,128)S(1)}, s32[16,16]{1,0:T(8,128)}, u32[]{:S(2)}) copy-start(s32[16,16]{1,0:T(8,128)} %param.35) | copy-start | bytes 3076
  202.2 14.4 %copy-start.13 = (f32[8]{0:T(128)S(1)}, f32[8]{0:T(128)}, u32[]{:S(2)}) copy-start(f32[8]{0:T(128)} %copy-done.12) | copy-start | bytes 100
  202.2 14.4 %copy-start.17 = (f32[8]{0:T(128)S(1)}, f32[8]{0:T(128)}, u32[]{:S(2)}) copy-start(f32[8]{0:T(128)} %copy-done.16) | copy-start | bytes 100
  202.2 14.4 %copy-start.21 = (f32[8]{0:T(128)S(1)}, f32[8]{0:T(128)}, u32[]{:S(2)}) copy-start(f32[8]{0:T(128)} %copy-done.20) | copy-start | bytes 100
  218.6 9.7 copy-start.4
  219.8 703.5 %collective-permute-start = (bf16[128,2,3,128]{3,2,1,0:T(4,128)(2,1)}, bf16[128,2,3,128]{3,2,1,0:T(4,128)(2,1)}, u32[]{:S(2)}, u32[]{:S(2)}) collective-permute-start(bf16[128,2,3,128]{3,2,1,0:T(4,128)(2,1)} %get-tuple-element.617), channel_id=1, source_target_pairs={{0,1},{1,2},{2,3},{3,4},{4,5},{5,6},{6,7},{8,9},{9,10},{10,11},{11... | collective-permute-start | bytes 589832 | tf_op jit(solution)/shard_map/ppermute | solution.py:16
  221.8 701.4 %collective-permute-start.1 = (bf16[128,2,3,128]{3,2,1,0:T(4,128)(2,1)}, bf16[128,2,3,128]{3,2,1,0:T(4,128)(2,1)}, u32[]{:S(2)}, u32[]{:S(2)}) collective-permute-start(bf16[128,2,3,128]{3,2,1,0:T(4,128)(2,1)} %get-tuple-element.618), channel_id=1, source_target_pairs={{1,0},{2,1},{3,2},{4,3},{5,4},{6,5},{7,6},{9,8},{10,9},{11,10},{12... | collective-permute-start | bytes 589832 | tf_op jit(solution)/shard_map/ppermute | solution.py:19
  937.2 12.2 collective-permute-start.2
  945.5 10.8 collective-permute-start.3
  (40 other events, 240.4 us)
where the time goes:
time: 1390 us; the launch traced here: 1370 us
  other arithmetic  649 us (47%)
  local copies, waits for them, and re-layouts  625 us (45%)
  matrix products  66.8 us (5%)
  starting transfers between devices  16.4 us (1%)
    gather x32, local copies, waits for them, and re-layouts, add_slot(): factor = jnp.take(flat_table, jnp.maximum(offset_col, 0), axis=0)  313 us
    add x32, other arithmetic, add_slot(): imag_total + factor_real * picked_imag + factor_imag * picked_real  239 us
    gather x32, local copies, waits for them, and re-layouts, add_slot(): picked = jnp.take(flat_patterns, jnp.maximum(source_col, 0), axis=0)  209 us
    slice x32, other arithmetic, add_slot(): factor_real = jnp.where(live_slot, factor[:, 0].astype(jnp.float32), 0.0)  136 us
    select_n x32, other arithmetic, add_slot(): picked = jnp.take(flat_patterns, jnp.maximum(source_col, 0), axis=0)  80.1 us
    reshape x2, local copies, waits for them, and re-layouts, translate(): flat_table = transfer_table.reshape(transfer_table.shape[0], 2, -1)  52.8 us
    reduce_sum x6, other arithmetic, shift_sum(): jnp.sum(child_terms[:, :, 0] * cosine - child_terms[:, :, 1] * sine, axis=1)  52.1 us
    dot_general x5, matrix products, parent_block(): jnp.einsum('pkcus,sv->pkcuv', halfway, azimuth_matrix, preferred_element_...  51.7 us
  transfers between devices with their start and end apart: 5, of which 0 were waited for; matrix products, arithmetic and copies ran while one was open for 55% of the time, Pallas kernels for 0%

commit v1 on v0

v1 whole, which is shorter than its diff:
```python
import math

import jax
import jax.numpy as jnp
import numpy as np
from jax import lax
from jax.experimental import pallas as pl
from jax.experimental.pallas import tpu as pltpu
from jax.sharding import PartitionSpec as P

VMEM_LIMIT = 58 * 1024 * 1024


def sample_angles(rows, cols):
    polar = (np.arange(rows) + 0.5) * (np.pi / rows)
    azimuth = np.arange(cols) * (2.0 * np.pi / cols)
    return polar, azimuth


def transverse_factors(rows, cols):
    polar, azimuth = sample_angles(rows, cols)
    first = rows / 8.0 * np.sin(polar)[:, None] * np.cos(azimuth)[None, :]
    second = rows / 8.0 * np.sin(polar)[:, None] * np.sin(azimuth)[None, :]
    return np.stack(
        [
            np.cos(first) * np.cos(second),
            np.sin(first) * np.cos(second),
            np.cos(first) * np.sin(second),
            np.sin(first) * np.sin(second),
        ]
    ).astype(np.float32)


def polar_operator(matrix, signs, chunk):
    rows, taps = matrix.shape
    polar, _ = sample_angles(rows, 1)
    axial = rows / 8.0 * np.cos(polar)
    in_phase = matrix.astype(jnp.float32) * np.cos(axial).astype(np.float32)[:, None]
    quadrature = matrix.astype(jnp.float32) * np.sin(axial).astype(np.float32)[:, None]
    real_row = []
    imag_row = []
    for sign in signs:
        real_row += [in_phase, -sign * quadrature]
        imag_row += [sign * quadrature, in_phase]
    whole = jnp.stack([jnp.concatenate(real_row, axis=1), jnp.concatenate(imag_row, axis=1)])
    whole = whole.reshape(2, rows // chunk, chunk, 2 * len(signs) * taps)
    whole = whole.transpose(1, 0, 2, 3)
    return whole.reshape(rows // chunk, 2 * chunk, -1).astype(jnp.bfloat16)


def aggregate_kernel(pairs, width, split, plain, x_ref, m_ref, b_ref, t_ref, *outs):
    parents = x_ref.shape[0]
    rows2, cols = x_ref.shape[3] * x_ref.shape[4], x_ref.shape[5]
    chunk = t_ref.shape[1]
    steps = b_ref.shape[1] // width
    out_plain = outs[0] if plain else None
    out_split = outs[-1] if split else None

    def one_parent(p):
        operator = m_ref[0, 0]
        halves = []
        for child in range(4):
            stacked = [x_ref[p, s, child].reshape(rows2, cols) for s in range(pairs)]
            stacked = stacked[0] if pairs == 1 else jnp.concatenate(stacked, axis=0)
            halves.append(stacked)
        joined = jnp.concatenate(halves, axis=1)
        h = jnp.dot(operator, joined, preferred_element_type=jnp.float32)
        h0, h1, h2, h3 = [h[:, k * cols : (k + 1) * cols] for k in range(4)]
        low_sum, low_diff = h0 + h1, h1 - h0
        high_sum, high_diff = h2 + h3, h3 - h2
        sums = jnp.concatenate(
            [
                (low_sum + high_sum).astype(jnp.bfloat16),
                (low_diff + high_diff).astype(jnp.bfloat16),
                (high_sum - low_sum).astype(jnp.bfloat16),
                (high_diff - low_diff).astype(jnp.bfloat16),
            ],
            axis=0,
        )

        def columns(j, start):
            cut = pl.ds(start, width)
            y = jnp.dot(sums, b_ref[:, cut], preferred_element_type=jnp.float32)
            part = [y[k * chunk : (k + 1) * chunk] for k in range(8)]
            f0, f1, f2, f3 = [t_ref[k, :, cut] for k in range(4)]
            real = f0 * part[0] - f1 * part[3] - f2 * part[5] - f3 * part[6]
            imag = f0 * part[1] + f1 * part[2] + f2 * part[4] - f3 * part[7]
            both = (real.astype(jnp.bfloat16), imag.astype(jnp.bfloat16))
            for c in range(2):
                if plain:
                    out_plain[p, c, :, cut] = both[c]
                if split:
                    band_rows, block_cols = out_split.shape[4], out_split.shape[5]
                    for q in range(width // block_cols):
                        for band in range(chunk // band_rows):
                            out_split[j * (width // block_cols) + q, band, p, c] = both[c][
                                band * band_rows : (band + 1) * band_rows,
                                q * block_cols : (q + 1) * block_cols,
                            ]

        if steps == 1:
            columns(0, 0)
        else:

            @pl.loop(0, steps)
            def _(j):
                columns(j, pl.multiple_of(j * width, width))

    if parents == 1:
        one_parent(0)
    else:

        @pl.loop(0, parents, unroll=2)
        def _(p):
            one_parent(p)


def aggregate(children, operator, azimuth, factors, group, plain, split, name):
    parents, pairs, _, _, taps, cols = children.shape
    per_parent, chunks, chunk2, depth = operator.shape
    chunk = chunk2 // 2
    rows, out_cols = factors.shape[1], factors.shape[2]
    width = min(256, out_cols)
    out_shape = []
    out_specs = []
    if plain:
        out_shape.append(jax.ShapeDtypeStruct((parents, 2, rows, out_cols), jnp.bfloat16))
        out_specs.append(pl.BlockSpec((group, 2, chunk, out_cols), lambda p, u: (p, 0, u, 0)))
    if split is not None:
        blocks, bands = split
        band_rows, block_cols = rows // bands, out_cols // blocks
        width = max(width, block_cols)
        out_shape.append(
            jax.ShapeDtypeStruct(
                (blocks, bands, parents, 2, band_rows, block_cols), jnp.bfloat16
            )
        )
        out_specs.append(
            pl.BlockSpec(
                (blocks, chunk // band_rows, group, 2, band_rows, block_cols),
                lambda p, u: (0, u, p, 0, 0, 0),
            )
        )

    def body(*refs):
        aggregate_kernel(pairs, width, split is not None, plain, *refs)

    if per_parent > 1:
        operator_map = lambda p, u: (p, u, 0, 0)
    else:
        operator_map = lambda p, u: (0, u, 0, 0)
    flops = 2 * parents * chunks * 4 * (chunk2 * depth * cols + chunk2 * cols * out_cols)
    moved = 2 * (children.size + parents * 2 * rows * out_cols) + 4 * factors.size
    return pl.pallas_call(
        body,
        grid=(parents // group, chunks),
        in_specs=[
            pl.BlockSpec((group, pairs, 4, 2, taps, cols), lambda p, u: (p, 0, 0, 0, 0, 0)),
            pl.BlockSpec((1, 1, chunk2, depth), operator_map),
            pl.BlockSpec(azimuth.shape, lambda p, u: (0, 0)),
            pl.BlockSpec((4, chunk, out_cols), lambda p, u: (0, u, 0)),
        ],
        out_specs=out_specs,
        out_shape=out_shape,
        compiler_params=pltpu.CompilerParams(vmem_limit_bytes=VMEM_LIMIT),
        cost_estimate=pl.CostEstimate(flops=flops, bytes_accessed=moved, transcendentals=0),
        name=name,
    )(children, operator, azimuth, factors)


def translate_kernel(slots, merge, src, off, cnt, x_ref, t_ref, o_ref, held):
    targets = o_ref.shape[0]
    sources = held.shape[0] - 1
    held[sources] = jnp.zeros(held.shape[1:], held.dtype)

    @pl.loop(0, sources, unroll=4)
    def _(s):
        if merge == 1:
            held[s] = x_ref[s]
        else:
            total = x_ref[s * merge].astype(jnp.float32)
            for k in range(1, merge):
                total = total + x_ref[s * merge + k].astype(jnp.float32)
            held[s] = total.astype(held.dtype)

    def gather(t, live):
        real = imag = None
        for first in range(0, live, 4):
            group_real = group_imag = None
            for j in range(first, min(first + 4, live)):
                picked = src[t * slots + j]
                chosen = off[t * slots + j]
                pr, pi = held[picked, 0], held[picked, 1]
                fr, fi = t_ref[chosen, 0], t_ref[chosen, 1]
                term_real = fr * pr - fi * pi
                term_imag = fr * pi + fi * pr
                group_real = term_real if group_real is None else group_real + term_real
                group_imag = term_imag if group_imag is None else group_imag + term_imag
            group_real = group_real.astype(jnp.float32)
            group_imag = group_imag.astype(jnp.float32)
            real = group_real if real is None else real + group_real
            imag = group_imag if imag is None else imag + group_imag
        o_ref[t, 0] = real.astype(o_ref.dtype)
        o_ref[t, 1] = imag.astype(o_ref.dtype)

    ends = sorted({min(slots, -(-slots * k // 16) * 4) for k in (2, 3)} | {slots})

    @pl.loop(0, targets)
    def _(t):
        live = cnt[t]
        lower = -1
        for end in ends:

            @pl.when(jnp.logical_and(live > lower, live <= end))
            def _(end=end):
                gather(t, end)

            lower = end


def translate(patterns, table, sources, displacements, row_chunk, merge, name):
    targets, slots = sources.shape
    displacement_count, _, rows, cols = table.shape
    incoming = patterns.shape[0]
    held_count = incoming // merge
    live = sources >= 0
    src = jnp.where(live, sources, held_count).reshape(-1)
    off = jnp.maximum(displacements, 0).reshape(-1)
    cnt = jnp.sum(live.astype(jnp.int32), axis=1)

    def body(*refs):
        translate_kernel(slots, merge, *refs)

    return pl.pallas_call(
        body,
        grid_spec=pltpu.PrefetchScalarGridSpec(
            num_scalar_prefetch=3,
            grid=(rows // row_chunk,),
            in_specs=[
                pl.BlockSpec((incoming, 2, row_chunk, cols), lambda r, *_: (0, 0, r, 0)),
                pl.BlockSpec((displacement_count, 2, row_chunk, cols), lambda r, *_: (0, 0, r, 0)),
            ],
            out_specs=pl.BlockSpec((targets, 2, row_chunk, cols), lambda r, *_: (0, 0, r, 0)),
            scratch_shapes=[pltpu.VMEM((held_count + 1, 2, row_chunk, cols), jnp.bfloat16)],
        ),
        out_shape=jax.ShapeDtypeStruct((targets, 2, rows, cols), jnp.bfloat16),
        compiler_params=pltpu.CompilerParams(vmem_limit_bytes=VMEM_LIMIT),
        cost_estimate=pl.CostEstimate(
            flops=8 * targets * slots * rows * cols,
            bytes_accessed=2 * (patterns.size + table.size),
            transcendentals=0,
        ),
        name=name,
    )(src, off, cnt, patterns, table)


def stencil_matrix(tap_index, weights, column_count):
    matches = (
        tap_index[:, :, None] == jnp.arange(column_count, dtype=jnp.int32)[None, None, :]
    ).astype(jnp.float32)
    return jnp.sum(weights.astype(jnp.float32)[:, :, None] * matches, axis=1)


def shards(
    patterns7,
    polar_up7,
    azimuth_up7,
    polar_up6,
    azimuth_up6,
    polar_first,
    polar_weights,
    azimuth_first,
    azimuth_weights,
    transfer5,
    sources5,
    offsets5,
    transfer4,
    sources4,
    offsets4,
):
    band_count = lax.axis_size("ang")
    block_count = lax.axis_size("clu")
    device_count = band_count * block_count
    device = lax.axis_index("clu") * band_count + lax.axis_index("ang")
    rows_six, cols_six = polar_up7.shape[0], azimuth_up7.shape[1]
    rows_five, cols_five = polar_up6.shape[0], azimuth_up6.shape[1]
    rows_four, cols_four = polar_first.shape[0], azimuth_first.shape[0]

    parents6 = patterns7.shape[0] // 8
    operator6 = polar_operator(polar_up7, (-1.0, 1.0), rows_six)[None]
    (level6,) = aggregate(
        patterns7.reshape((parents6, 2, 4) + patterns7.shape[1:]),
        operator6,
        azimuth_up7,
        transverse_factors(rows_six, cols_six),
        math.gcd(parents6, 8),
        True,
        None,
        "level6",
    )

    parents5 = parents6 // 8
    operator5 = polar_operator(polar_up6, (-1.0, 1.0), rows_five // 2)[None]
    level5, windows5 = aggregate(
        level6.reshape((parents5, 2, 4) + level6.shape[1:]),
        operator5,
        azimuth_up6,
        transverse_factors(rows_five, cols_five),
        1,
        True,
        (block_count, band_count),
        "level5",
    )
    windows5 = windows5.reshape((device_count,) + windows5.shape[2:])
    arrived5 = lax.all_to_all(windows5, ("clu", "ang"), 0, 0, tiled=True)
    arrived5 = arrived5.reshape((device_count * parents5,) + arrived5.shape[2:])

    four_taps = jnp.arange(4, dtype=jnp.int32)[None, :]
    polar_matrix = stencil_matrix(polar_first[:, None] + four_taps, polar_weights, rows_five)
    azimuth_matrix = stencil_matrix(
        (azimuth_first[:, None] + four_taps) % cols_five, azimuth_weights, cols_five
    ).T.astype(jnp.bfloat16)
    parts = parents5 // 4
    operators4 = []
    for part in range(parts):
        sign = (2 * ((device * parts + part) % 2) - 1).astype(jnp.float32)
        operators4.append(polar_operator(polar_matrix, (sign,), rows_four // 4))
    (windows4,) = aggregate(
        level5.reshape((parts, 1, 4) + level5.shape[1:]),
        jnp.stack(operators4),
        azimuth_matrix,
        transverse_factors(rows_four, cols_four),
        1,
        False,
        (block_count, band_count),
        "level4",
    )
    windows4 = windows4.reshape((device_count,) + windows4.shape[2:])
    arrived4 = lax.all_to_all(windows4, ("clu", "ang"), 0, 0, tiled=True)
    arrived4 = arrived4.reshape((device_count * parts,) + arrived4.shape[2:])

    translated5 = translate(
        arrived5, transfer5, sources5, offsets5, transfer5.shape[2], 1, "translate5"
    )
    translated4 = translate(arrived4, transfer4, sources4, offsets4, 16, 2, "translate4")
    return translated5, translated4


def solution(mesh):
    in_specs = (
        P(("clu", "ang"), None, None, None),
        P(),
        P(),
        P(),
        P(),
        P(),
        P(),
        P(),
        P(),
        P(None, None, "ang", "clu"),
        P(),
        P(),
        P(None, None, "ang", "clu"),
        P(),
        P(),
    )
    out_specs = (P(None, None, "ang", "clu"), P(None, None, "ang", "clu"))
    return jax.shard_map(shards, mesh=mesh, in_specs=in_specs, out_specs=out_specs, check_vma=False)
```

time: 1390 us -> 153 us (0.11); the launches traced: 1370 us -> 151 us
  other arithmetic: 649 us -> 7.48 us
  local copies, waits for them, and re-layouts: 625 us -> 6.35 us
  Pallas kernels: 0 us -> 70 us
  matrix products: 66.8 us -> 0 us
  waiting for transfers between devices: 0.01 us -> 55.8 us
    gather x64 -> x0, local copies, waits for them, and re-layouts: 522 us -> none  [the longest x32 313 us: add_slot(): factor = jnp.take(flat_table, jnp.maximum(offset_col, 0), axis=0)]
    add x35 -> x1, other arithmetic: 240 us -> 0.01 us  [shards(): polar_first[:, None] + four_taps]
    slice x32 -> x0, other arithmetic: 136 us -> none  [add_slot(): factor_real = jnp.where(live_slot, factor[:, 0].astype(jnp.float32), 0.0)]
    select_n x65 -> x1, other arithmetic: 130 us -> 0.02 us  [shards(): (azimuth_first[:, None] + four_taps) % cols_five]
    pallas_call x0 -> x5, Pallas kernels: none -> 70 us  [the longest x3 40.9 us: aggregate(): pl.pallas_call(body, grid=(parents // group, chunks), in_specs=[pl.BlockS...]
    dot_general x7 -> x0, matrix products: 66.8 us -> none  [the longest x5 51.7 us: parent_block(): jnp.einsum('pkcus,sv->pkcuv', halfway, azimuth_matrix, preferred_element_...]
    all_to_all x1 -> x2, waiting for transfers between devices: 0.01 us -> 55.8 us  [the longest x1 29.3 us: shards(): arrived5 = lax.all_to_all(windows5, ('clu', 'ang'), 0, 0, tiled=True)]
    reshape x3 -> x4, local copies, waits for them, and re-layouts: 54.6 us -> 2.69 us  [the longest x2 1.35 us: translate(): off = jnp.maximum(displacements, 0).reshape(-1)]
  transfers between devices with their start and end apart: 5 -> 2, of which waited for: 0 -> 2; matrix products, arithmetic and copies ran while one was open for 55% -> 6% of each run, Pallas kernels for 0% -> 21%
where the time goes in v1:
time: 153 us; the launch traced here: 151 us
  Pallas kernels  70 us (46%)
  waiting for transfers between devices  55.8 us (36%)
  starting transfers between devices  10.7 us (7%)
  other arithmetic  7.48 us (5%)
  local copies, waits for them, and re-layouts  6.35 us (4%)
    pallas_call x3, Pallas kernels, aggregate(): pl.pallas_call(body, grid=(parents // group, chunks), in_specs=[pl.BlockS...  40.9 us
    all_to_all x1, waiting for transfers between devices, shards(): arrived5 = lax.all_to_all(windows5, ('clu', 'ang'), 0, 0, tiled=True)  29.3 us
    pallas_call x2, Pallas kernels, translate(): pl.pallas_call(body, grid_spec=pltpu.PrefetchScalarGridSpec(num_scalar_pr...  29.1 us
    all_to_all x1, waiting for transfers between devices, shards(): arrived4 = lax.all_to_all(windows4, ('clu', 'ang'), 0, 0, tiled=True)  26.5 us
    all_to_all x1, starting transfers between devices, shards(): arrived5 = lax.all_to_all(windows5, ('clu', 'ang'), 0, 0, tiled=True)  6.12 us
    all_to_all x1, starting transfers between devices, shards(): arrived4 = lax.all_to_all(windows4, ('clu', 'ang'), 0, 0, tiled=True)  4.54 us
  transfers between devices with their start and end apart: 2, of which 2 were waited for; matrix products, arithmetic and copies ran while one was open for 6% of the time, Pallas kernels for 21%

profile of v1, /device:TPU:4, one launch (start us, length us, event | category | flops | bytes accessed | tf_op | source)
XLA Modules:
  0.0 151.1 jit_solution(7938928474033801760)
XLA Ops:
  0.6 0.7 fusion.6
  1.4 0.8 copy.48
  2.2 1.0 fusion.2
  3.2 0.8 pad_maximum_fusion
  4.1 13.4 %level6.1 = bf16[32,2,128,256]{3,2,1,0:T(8,128)(2,1)} custom-call(bf16[32,2,4,2,64,128]{5,4,3,2,1,0:T(8,128)(2,1)} %bitcast.42, bf16[1,1,256,256]{3,2,1,0:T(8,128)(2,1)} %bitcast.41, bf16[128,256]{1,0:T(8,128)(2,1)} %refs_2_.2, f32[4,128,256]{2,1,0:T(8,128)} %constant.74.clone.refs_3_), custom_call_target="tpu_custom_call" | custom-call | flops 4294967296 | bytes 13107200 | tf_op jit(solution)/shard_map/level6/pallas_call | solution.py:154
  17.4 13.6 %level5.1 = (bf16[4,2,256,512]{3,2,1,0:T(8,128)(2,1)}, bf16[4,8,4,2,32,128]{5,4,3,2,1,0:T(8,128)(2,1)}) custom-call(bf16[4,2,4,2,128,256]{5,4,3,2,1,0:T(8,128)(2,1)} %bitcast.43, bf16[1,2,256,512]{3,2,1,0:T(8,128)(2,1)} %bitcast.40, bf16[256,512]{1,0:T(8,128)(2,1)} %refs_2_.3, f32[4,256,512]{2,1,0:T(8,128)} %constant.77.clone.refs_3_), custom_call_target="tpu_custom_call" | custom-call | flops 4294967296 | bytes 8388608 | tf_op jit(solution)/shard_map/level5/pallas_call | solution.py:154
  31.1 6.1 %all-to-all-start = ((bf16[32,4,2,32,128]{4,3,2,1,0:T(8,128)(2,1)}), bf16[32,4,2,32,128]{4,3,2,1,0:T(8,128)(2,1)S(1)}, u32[]{:S(2)}, u32[]{:S(2)}) async-start(bf16[32,4,2,32,128]{4,3,2,1,0:T(8,128)(2,1)} %bitcast.33), calls=%async_computation | async-start | bytes 4194304 | tf_op jit(solution)/shard_map/all_to_all | solution.py:315
  37.3 1.6 %select_reduce_fusion = bf16[1024,512]{1,0:T(8,128)(2,1)S(1)} fusion(f32[1024,4]{0,1:T(4,128)S(1)} %convert_element_type.82, s32[1024,4]{0,1:T(4,128)S(1)} %add_select_fusion), kind=kLoop, calls=%fused_computation | loop fusion | flops 5767168 | bytes 1081344 | tf_op jit(solution)/shard_map/reduce_sum | solution.py:261
  39.0 1.3 copy.53
  40.3 0.7 select_reduce_fusion.1
  41.3 1.1 maximum_maximum_fusion
  42.3 13.9 %level4.1 = bf16[4,8,1,2,64,256]{5,4,3,2,1,0:T(8,128)(2,1)} custom-call(bf16[1,1,4,2,256,512]{5,4,3,2,1,0:T(8,128)(2,1)} %bitcast.44, bf16[1,4,256,512]{3,2,1,0:T(8,128)(2,1)} %bitcast.36, bf16[512,1024]{1,0:T(8,128)(2,1)} %bitcast.37, f32[4,512,1024]{2,1,0:T(8,128)} %constant.80.clone.refs_3_), custom_call_target="tpu_custom_call" | custom-call | flops 6442450944 | bytes 12582912 | tf_op jit(solution)/shard_map/level4/pallas_call | solution.py:154
  56.3 29.3 %all-to-all-done = bf16[32,4,2,32,128]{4,3,2,1,0:T(8,128)(2,1)S(1)} async-done(((bf16[32,4,2,32,128]{4,3,2,1,0:T(8,128)(2,1)}), bf16[32,4,2,32,128]{4,3,2,1,0:T(8,128)(2,1)S(1)}, u32[]{:S(2)}, u32[]{:S(2)}) %all-to-all-start) | async-done | bytes 2097184 | tf_op jit(solution)/shard_map/all_to_all | solution.py:315
  85.6 1.3 copy-done
  86.9 4.5 %all-to-all-start.1 = ((bf16[32,1,2,64,256]{4,3,2,1,0:T(8,128)(2,1)}), bf16[32,1,2,64,256]{4,3,2,1,0:T(8,128)(2,1)}, u32[]{:S(2)}, u32[]{:S(2)}) async-start(bf16[32,1,2,64,256]{4,3,2,1,0:T(8,128)(2,1)} %bitcast.34), calls=%async_computation.1 | async-start | bytes 4194304 | tf_op jit(solution)/shard_map/all_to_all | solution.py:339
  91.5 0.6 fusion.9
  92.2 0.7 reshape.196.refs_0_
  92.9 0.7 reshape.197.refs_1_
  93.6 0.6 fusion.10
  94.2 0.7 reshape.202.refs_0_
  94.9 0.7 reshape.203.refs_1_
  95.6 17.9 %translate5.1 = bf16[128,2,32,128]{3,2,1,0:T(8,128)(2,1)} custom-call(s32[2048]{0:T(1024)} %reshape.196.refs_0_, s32[2048]{0:T(1024)} %reshape.197.refs_1_, s32[128]{0:T(128)} %get-tuple-element.21.refs_2_, bf16[128,2,32,128]{3,2,1,0:T(8,128)(2,1)} %bitcast.32, bf16[316,2,32,128]{3,2,1,0:T(8,128)(2,1)} %refs_4_.2), custom_call_target="tpu_custom_call" | custom-call | flops 67108864 | bytes 7274496 | tf_op jit(solution)/shard_map/translate5/pallas_call | solution.py:234
  113.5 26.5 %all-to-all-done.1 = bf16[32,1,2,64,256]{4,3,2,1,0:T(8,128)(2,1)} async-done(((bf16[32,1,2,64,256]{4,3,2,1,0:T(8,128)(2,1)}), bf16[32,1,2,64,256]{4,3,2,1,0:T(8,128)(2,1)}, u32[]{:S(2)}, u32[]{:S(2)}) %all-to-all-start.1) | async-done | bytes 2097184 | tf_op jit(solution)/shard_map/all_to_all | solution.py:339
  140.0 11.1 %translate4.1 = bf16[16,2,64,256]{3,2,1,0:T(8,128)(2,1)} custom-call(s32[256]{0:T(256)} %reshape.202.refs_0_, s32[256]{0:T(256)} %reshape.203.refs_1_, s32[16]{0:T(128)} %get-tuple-element.19.refs_2_, bf16[32,2,64,256]{3,2,1,0:T(8,128)(2,1)} %bitcast.22.refs_3_, bf16[316,2,64,256]{3,2,1,0:T(8,128)(2,1)} %refs_4_.3), custom_call_target="tpu_custom_call" | custom-call | flops 33554432 | bytes 22806528 | tf_op jit(solution)/shard_map/translate4/pallas_call | solution.py:234
  (33 shorter events, 0.6 us)
Async XLA Ops:
  31.0 6.2 %copy-start.6 = (bf16[512,4]{0,1:T(4,128)(2,1)S(1)}, bf16[512,4]{0,1:T(4,128)(2,1)}, u32[]{:S(2)}) copy-start(bf16[512,4]{0,1:T(4,128)(2,1)} %param.30) | copy-start | bytes 12292
  31.0 6.2 %copy-start.1 = (bf16[1024,4]{0,1:T(4,128)(2,1)S(1)}, bf16[1024,4]{0,1:T(4,128)(2,1)}, u32[]{:S(2)}) copy-start(bf16[1024,4]{0,1:T(4,128)(2,1)} %param.32) | copy-start | bytes 24580
  31.1 6.3 %copy-start.7 = (s32[1024]{0:T(1024)S(1)}, s32[1024]{0:T(1024)}, u32[]{:S(2)}) copy-start(s32[1024]{0:T(1024)} %param.31) | copy-start | bytes 12292
  31.1 54.5 %all-to-all-start = ((bf16[32,4,2,32,128]{4,3,2,1,0:T(8,128)(2,1)}), bf16[32,4,2,32,128]{4,3,2,1,0:T(8,128)(2,1)S(1)}, u32[]{:S(2)}, u32[]{:S(2)}) async-start(bf16[32,4,2,32,128]{4,3,2,1,0:T(8,128)(2,1)} %bitcast.33), calls=%async_computation | async-start | bytes 4194304 | tf_op jit(solution)/shard_map/all_to_all | solution.py:315
  37.2 3.1 %copy-start.10 = (s32[512]{0:T(512)S(1)}, s32[512]{0:T(512)}, u32[]{:S(2)}) copy-start(s32[512]{0:T(512)} %param.29) | copy-start | bytes 6148
  37.2 3.8 %copy-start.8 = (f32[4,128]{1,0:T(4,128)S(1)}, f32[4,128]{1,0:T(4,128)}, u32[]{:S(2)}) copy-start(f32[4,128]{1,0:T(4,128)} %constant.86) | copy-start | bytes 6148
  37.2 3.8 %copy-start.9 = (f32[4,128]{1,0:T(4,128)S(1)}, f32[4,128]{1,0:T(4,128)}, u32[]{:S(2)}) copy-start(f32[4,128]{1,0:T(4,128)} %constant.85) | copy-start | bytes 6148
  85.6 1.3 copy-start
  85.6 5.9 %copy-start.2 = (s32[128,16]{0,1:T(8,128)S(1)}, s32[128,16]{0,1:T(8,128)}, u32[]{:S(2)}) copy-start(s32[128,16]{0,1:T(8,128)} %param.34) | copy-start | bytes 24580
  85.6 7.2 %copy-start.3 = (s32[128,16]{0,1:T(8,128)S(1)}, s32[128,16]{0,1:T(8,128)}, u32[]{:S(2)}) copy-start(s32[128,16]{0,1:T(8,128)} %param.35) | copy-start | bytes 24580
  85.6 8.0 %copy-start.4 = (s32[16,16]{1,0:T(8,128)S(1)}, s32[16,16]{1,0:T(8,128)}, u32[]{:S(2)}) copy-start(s32[16,16]{1,0:T(8,128)} %param.37) | copy-start | bytes 3076
  85.6 9.3 %copy-start.5 = (s32[16,16]{1,0:T(8,128)S(1)}, s32[16,16]{1,0:T(8,128)}, u32[]{:S(2)}) copy-start(s32[16,16]{1,0:T(8,128)} %param.38) | copy-start | bytes 3076
  86.9 53.0 %all-to-all-start.1 = ((bf16[32,1,2,64,256]{4,3,2,1,0:T(8,128)(2,1)}), bf16[32,1,2,64,256]{4,3,2,1,0:T(8,128)(2,1)}, u32[]{:S(2)}, u32[]{:S(2)}) async-start(bf16[32,1,2,64,256]{4,3,2,1,0:T(8,128)(2,1)} %bitcast.34), calls=%async_computation.1 | async-start | bytes 4194304 | tf_op jit(solution)/shard_map/all_to_all | solution.py:339

commit v2 on v1

v2 whole, which is shorter than its diff:
```python
import math

import jax
import jax.numpy as jnp
import numpy as np
from jax import lax
from jax.experimental import pallas as pl
from jax.experimental.pallas import tpu as pltpu
from jax.sharding import PartitionSpec as P

VMEM_LIMIT = 58 * 1024 * 1024
REGROUPS = 2


def sample_angles(rows, cols):
    polar = (np.arange(rows) + 0.5) * (np.pi / rows)
    azimuth = np.arange(cols) * (2.0 * np.pi / cols)
    return polar, azimuth


def transverse_factors(rows, cols):
    polar, azimuth = sample_angles(rows, cols)
    first = rows / 8.0 * np.sin(polar)[:, None] * np.cos(azimuth)[None, :]
    second = rows / 8.0 * np.sin(polar)[:, None] * np.sin(azimuth)[None, :]
    return np.stack(
        [
            np.cos(first) * np.cos(second),
            np.sin(first) * np.cos(second),
            np.cos(first) * np.sin(second),
            np.sin(first) * np.sin(second),
        ]
    ).astype(np.float32)


def polar_operator(matrix, signs, chunk):
    rows, taps = matrix.shape
    polar, _ = sample_angles(rows, 1)
    axial = rows / 8.0 * np.cos(polar)
    in_phase = matrix.astype(jnp.float32) * np.cos(axial).astype(np.float32)[:, None]
    quadrature = matrix.astype(jnp.float32) * np.sin(axial).astype(np.float32)[:, None]
    real_row = []
    imag_row = []
    for sign in signs:
        real_row += [in_phase, -sign * quadrature]
        imag_row += [sign * quadrature, in_phase]
    whole = jnp.stack([jnp.concatenate(real_row, axis=1), jnp.concatenate(imag_row, axis=1)])
    whole = whole.reshape(2, rows // chunk, chunk, 2 * len(signs) * taps)
    whole = whole.transpose(1, 0, 2, 3)
    return whole.reshape(rows // chunk, 2 * chunk, -1).astype(jnp.bfloat16)


def sign_sums(h, cols):
    h0, h1, h2, h3 = [h[:, k * cols : (k + 1) * cols] for k in range(4)]
    low_sum, low_diff = h0 + h1, h1 - h0
    high_sum, high_diff = h2 + h3, h3 - h2
    return jnp.concatenate(
        [
            (low_sum + high_sum).astype(jnp.bfloat16),
            (low_diff + high_diff).astype(jnp.bfloat16),
            (high_sum - low_sum).astype(jnp.bfloat16),
            (high_diff - low_diff).astype(jnp.bfloat16),
        ],
        axis=0,
    )


def apply_factors(y, chunk, factors):
    part = [y[k * chunk : (k + 1) * chunk] for k in range(8)]
    f0, f1, f2, f3 = factors
    real = f0 * part[0] - f1 * part[3] - f2 * part[5] - f3 * part[6]
    imag = f0 * part[1] + f1 * part[2] + f2 * part[4] - f3 * part[7]
    return real.astype(jnp.bfloat16), imag.astype(jnp.bfloat16)


def aggregate_kernel(pairs, width, split, x_ref, m_ref, b_ref, t_ref, o_ref):
    parents = x_ref.shape[0]
    rows2, cols = x_ref.shape[3] * x_ref.shape[4], x_ref.shape[5]
    chunk = t_ref.shape[1]
    steps = b_ref.shape[1] // width

    def one_parent(p):
        halves = []
        for child in range(4):
            stacked = [x_ref[p, s, child].reshape(rows2, cols) for s in range(pairs)]
            halves.append(jnp.concatenate(stacked, axis=0))
        joined = jnp.concatenate(halves, axis=1)
        h = jnp.dot(m_ref[0], joined, preferred_element_type=jnp.float32)
        sums = sign_sums(h, cols)

        def columns(j, start):
            cut = pl.ds(start, width)
            y = jnp.dot(sums, b_ref[:, cut], preferred_element_type=jnp.float32)
            both = apply_factors(y, chunk, [t_ref[k, :, cut] for k in range(4)])
            for c in range(2):
                if split:
                    band_rows, block_cols = o_ref.shape[4], o_ref.shape[5]
                    for q in range(width // block_cols):
                        for band in range(chunk // band_rows):
                            o_ref[j * (width // block_cols) + q, band, p, c] = both[c][
                                band * band_rows : (band + 1) * band_rows,
                                q * block_cols : (q + 1) * block_cols,
                            ]
                else:
                    o_ref[p, c, :, cut] = both[c]

        if steps == 1:
            columns(0, 0)
        else:

            @pl.loop(0, steps)
            def _(j):
                columns(j, pl.multiple_of(j * width, width))

    if parents == 1:
        one_parent(0)
    else:

        @pl.loop(0, parents, unroll=2)
        def _(p):
            one_parent(p)


def aggregate(children, operator, azimuth, factors, first, parents, group, split, name):
    _, pairs, _, _, taps, cols = children.shape
    chunks, chunk2, depth = operator.shape
    chunk = chunk2 // 2
    rows, out_cols = factors.shape[1], factors.shape[2]
    width = min(256, out_cols)
    if split is None:
        out_shape = jax.ShapeDtypeStruct((parents, 2, rows, out_cols), jnp.bfloat16)
        out_spec = pl.BlockSpec((group, 2, chunk, out_cols), lambda p, u: (p, 0, u, 0))
    else:
        blocks, bands = split
        band_rows, block_cols = rows // bands, out_cols // blocks
        width = max(width, block_cols)
        out_shape = jax.ShapeDtypeStruct(
            (blocks, bands, parents, 2, band_rows, block_cols), jnp.bfloat16
        )
        out_spec = pl.BlockSpec(
            (blocks, chunk // band_rows, group, 2, band_rows, block_cols),
            lambda p, u: (0, u, p, 0, 0, 0),
        )

    def body(*refs):
        aggregate_kernel(pairs, width, split is not None, *refs)

    skip = first // group
    flops = 2 * parents * chunks * 4 * (chunk2 * depth * cols + chunk2 * cols * out_cols)
    moved = 2 * parents * (16 * taps * cols + 2 * rows * out_cols) + 4 * factors.size
    return pl.pallas_call(
        body,
        grid=(parents // group, chunks),
        in_specs=[
            pl.BlockSpec((group, pairs, 4, 2, taps, cols), lambda p, u: (p + skip, 0, 0, 0, 0, 0)),
            pl.BlockSpec((1, chunk2, depth), lambda p, u: (u, 0, 0)),
            pl.BlockSpec(azimuth.shape, lambda p, u: (0, 0)),
            pl.BlockSpec((4, chunk, out_cols), lambda p, u: (0, u, 0)),
        ],
        out_specs=out_spec,
        out_shape=out_shape,
        compiler_params=pltpu.CompilerParams(vmem_limit_bytes=VMEM_LIMIT),
        cost_estimate=pl.CostEstimate(flops=flops, bytes_accessed=moved, transcendentals=0),
        name=name,
    )(children, operator, azimuth, factors)


def halfway_kernel(m_ref, e_ref, *refs):
    *inputs, h_ref, g_ref = refs
    count = len(inputs) // 2
    parents, _, held, _, rows, cols = inputs[0].shape
    edge_rows = inputs[count].shape[4]

    @pl.loop(0, parents, unroll=2)
    def _(p):
        siblings = []
        for c in range(count):
            for i in range(held):
                pieces = [inputs[c][p, s, i].reshape(2 * rows, cols) for s in range(2)]
                pieces += [
                    inputs[count + c][p, s, i].reshape(2 * edge_rows, cols) for s in range(2)
                ]
                siblings.append(jnp.concatenate(pieces, axis=0))
        joined = jnp.concatenate(siblings, axis=1)
        h = jnp.dot(m_ref[...], joined, preferred_element_type=jnp.float32)
        sums = sign_sums(h, cols)
        h_ref[p] = sums
        edges = lax.dot_general(
            e_ref[...], sums, (((1,), (1,)), ((), ())), preferred_element_type=jnp.float32
        )
        g_ref[p] = edges.astype(jnp.bfloat16)


def halfway(mains, edges, operator, picker):
    count = len(mains)
    parents, _, held, _, rows, cols = mains[0].shape
    edge_rows = edges[0].shape[4]
    group = math.gcd(parents, 4)
    out_rows = 4 * operator.shape[0]
    return pl.pallas_call(
        halfway_kernel,
        grid=(parents // group,),
        in_specs=[
            pl.BlockSpec(operator.shape, lambda p: (0, 0)),
            pl.BlockSpec(picker.shape, lambda p: (0, 0)),
        ]
        + [pl.BlockSpec((group, 2, held, 2, rows, cols), lambda p: (p, 0, 0, 0, 0, 0))] * count
        + [pl.BlockSpec((group, 2, held, 2, edge_rows, cols), lambda p: (p, 0, 0, 0, 0, 0))]
        * count,
        out_specs=[
            pl.BlockSpec((group, out_rows, cols), lambda p: (p, 0, 0)),
            pl.BlockSpec((group, picker.shape[0], out_rows), lambda p: (p, 0, 0)),
        ],
        out_shape=[
            jax.ShapeDtypeStruct((parents, out_rows, cols), jnp.bfloat16),
            jax.ShapeDtypeStruct((parents, picker.shape[0], out_rows), jnp.bfloat16),
        ],
        compiler_params=pltpu.CompilerParams(vmem_limit_bytes=VMEM_LIMIT),
        cost_estimate=pl.CostEstimate(
            flops=2 * parents * operator.size * 4 * cols,
            bytes_accessed=4 * parents * out_rows * cols,
            transcendentals=0,
        ),
        name="halfway4",
    )(operator, picker, *mains, *edges)


def phi_kernel(h_ref, low_ref, high_ref, b_ref, e_ref, t_ref, o_ref):
    parents = h_ref.shape[0]
    chunk = t_ref.shape[1]

    @pl.loop(0, parents, unroll=2)
    def _(p):
        outside = jnp.concatenate([low_ref[p], high_ref[p]], axis=0)
        y = jnp.dot(h_ref[p], b_ref[...], preferred_element_type=jnp.float32)
        y = y + lax.dot_general(
            outside, e_ref[...], (((0,), (0,)), ((), ())), preferred_element_type=jnp.float32
        )
        both = apply_factors(y, chunk, [t_ref[k] for k in range(4)])
        for c in range(2):
            o_ref[p, c] = both[c]


def interpolate_phi(h, low, high, azimuth, azimuth_edge, factors):
    parents, rows8, cols = h.shape
    _, rows, out_cols = factors.shape
    group = math.gcd(parents, 4)
    edge_spec = pl.BlockSpec((group,) + low.shape[1:], lambda p: (p, 0, 0))
    return pl.pallas_call(
        phi_kernel,
        grid=(parents // group,),
        in_specs=[
            pl.BlockSpec((group, rows8, cols), lambda p: (p, 0, 0)),
            edge_spec,
            edge_spec,
            pl.BlockSpec(azimuth.shape, lambda p: (0, 0)),
            pl.BlockSpec(azimuth_edge.shape, lambda p: (0, 0)),
            pl.BlockSpec(factors.shape, lambda p: (0, 0, 0)),
        ],
        out_specs=pl.BlockSpec((group, 2, rows, out_cols), lambda p: (p, 0, 0, 0)),
        out_shape=jax.ShapeDtypeStruct((parents, 2, rows, out_cols), jnp.bfloat16),
        compiler_params=pltpu.CompilerParams(vmem_limit_bytes=VMEM_LIMIT),
        cost_estimate=pl.CostEstimate(
            flops=2 * parents * rows8 * (cols + 16) * out_cols,
            bytes_accessed=4 * parents * rows8 * cols,
            transcendentals=0,
        ),
        name="level4",
    )(h, low, high, azimuth, azimuth_edge, factors)


def translate_kernel(slots, src, off, cnt, t_ref, *refs):
    *inputs, o_ref, held = refs
    targets = o_ref.shape[0]
    sources = held.shape[0] - 1
    senders, part = inputs[0].shape[:2]
    held[sources] = jnp.zeros(held.shape[1:], held.dtype)

    @pl.loop(0, senders)
    def _(s):
        for c, x_ref in enumerate(inputs):
            for i in range(part):
                held[(s * len(inputs) + c) * part + i] = x_ref[s, i]

    def gather(t, live):
        real = imag = None
        for first in range(0, live, 4):
            group_real = group_imag = None
            for j in range(first, min(first + 4, live)):
                picked = src[t * slots + j]
                chosen = off[t * slots + j]
                pr, pi = held[picked, 0], held[picked, 1]
                fr, fi = t_ref[chosen, 0], t_ref[chosen, 1]
                term_real = fr * pr - fi * pi
                term_imag = fr * pi + fi * pr
                group_real = term_real if group_real is None else group_real + term_real
                group_imag = term_imag if group_imag is None else group_imag + term_imag
            group_real = group_real.astype(jnp.float32)
            group_imag = group_imag.astype(jnp.float32)
            real = group_real if real is None else real + group_real
            imag = group_imag if imag is None else imag + group_imag
        o_ref[t, 0] = real.astype(o_ref.dtype)
        o_ref[t, 1] = imag.astype(o_ref.dtype)

    ends = sorted({min(slots, -(-slots * k // 16) * 4) for k in (2, 3)} | {slots})

    @pl.loop(0, targets)
    def _(t):
        live = cnt[t]
        lower = -1
        for end in ends:

            @pl.when(jnp.logical_and(live > lower, live <= end))
            def _(end=end):
                gather(t, end)

            lower = end


def translate(patterns, table, sources, displacements, row_chunk, name):
    targets, slots = sources.shape
    displacement_count, _, rows, cols = table.shape
    senders, part = patterns[0].shape[:2]
    held_count = senders * part * len(patterns)
    live = sources >= 0
    src = jnp.where(live, sources, held_count).reshape(-1)
    off = jnp.maximum(displacements, 0).reshape(-1)
    cnt = jnp.sum(live.astype(jnp.int32), axis=1)

    def body(*refs):
        translate_kernel(slots, *refs)

    return pl.pallas_call(
        body,
        grid_spec=pltpu.PrefetchScalarGridSpec(
            num_scalar_prefetch=3,
            grid=(rows // row_chunk,),
            in_specs=[
                pl.BlockSpec((displacement_count, 2, row_chunk, cols), lambda r, *_: (0, 0, r, 0)),
            ]
            + [pl.BlockSpec((senders, part, 2, row_chunk, cols), lambda r, *_: (0, 0, 0, r, 0))]
            * len(patterns),
            out_specs=pl.BlockSpec((targets, 2, row_chunk, cols), lambda r, *_: (0, 0, r, 0)),
            scratch_shapes=[pltpu.VMEM((held_count + 1, 2, row_chunk, cols), jnp.bfloat16)],
        ),
        out_shape=jax.ShapeDtypeStruct((targets, 2, rows, cols), jnp.bfloat16),
        compiler_params=pltpu.CompilerParams(vmem_limit_bytes=VMEM_LIMIT),
        cost_estimate=pl.CostEstimate(
            flops=8 * targets * slots * rows * cols,
            bytes_accessed=2 * (2 * targets * 2 * rows * cols + table.size),
            transcendentals=0,
        ),
        name=name,
    )(src, off, cnt, table, *patterns)


def stencil_matrix(tap_index, weights, column_count):
    matches = (
        tap_index[:, :, None] == jnp.arange(column_count, dtype=jnp.int32)[None, None, :]
    ).astype(jnp.float32)
    return jnp.sum(weights.astype(jnp.float32)[:, :, None] * matches, axis=1)


def shards(
    patterns7,
    polar_up7,
    azimuth_up7,
    polar_up6,
    azimuth_up6,
    polar_first,
    polar_weights,
    azimuth_first,
    azimuth_weights,
    transfer5,
    sources5,
    offsets5,
    transfer4,
    sources4,
    offsets4,
):
    band_count = lax.axis_size("ang")
    block_count = lax.axis_size("clu")
    device_count = band_count * block_count
    band = lax.axis_index("ang")
    block = lax.axis_index("clu")
    rows_six, cols_six = polar_up7.shape[0], azimuth_up7.shape[1]
    rows_five, cols_five = polar_up6.shape[0], azimuth_up6.shape[1]
    rows_four, cols_four = polar_first.shape[0], azimuth_first.shape[0]
    source_rows, source_cols = rows_five // band_count, cols_five // block_count
    band_rows, block_cols = rows_four // band_count, cols_four // block_count

    parents6 = patterns7.shape[0] // 8
    parents5 = parents6 // 8
    assert parents5 == 4
    part = parents5 // REGROUPS
    operator6 = polar_operator(polar_up7, (-1.0, 1.0), rows_six)
    operator5 = polar_operator(polar_up6, (-1.0, 1.0), rows_five // 2)
    children7 = patterns7.reshape((parents6, 2, 4) + patterns7.shape[1:])
    arrived5 = []
    for step in range(REGROUPS):
        level6 = aggregate(
            children7,
            operator6,
            azimuth_up7,
            transverse_factors(rows_six, cols_six),
            step * part * 8,
            part * 8,
            8,
            None,
            "level6",
        )
        windows5 = aggregate(
            level6.reshape((part, 2, 4) + level6.shape[1:]),
            operator5,
            azimuth_up6,
            transverse_factors(rows_five, cols_five),
            0,
            part,
            1,
            (block_count, band_count),
            "level5",
        )
        windows5 = windows5.reshape((device_count,) + windows5.shape[2:])
        arrived5.append(lax.all_to_all(windows5, ("clu", "ang"), 0, 0, tiled=True))

    upward = [(i, i + 1) for i in range(band_count - 1)]
    downward = [(i + 1, i) for i in range(band_count - 1)]
    edges5 = []
    for arrived in arrived5:
        low = lax.ppermute(arrived[:, :, :, source_rows - 3 :], "ang", upward)
        high = lax.ppermute(arrived[:, :, :, :3], "ang", downward)
        fill = jnp.zeros(arrived.shape[:3] + (10, source_cols), jnp.bfloat16)
        edges5.append(jnp.concatenate([low, high, fill], axis=3))

    four_taps = jnp.arange(4, dtype=jnp.int32)[None, :]
    polar_local = (
        lax.dynamic_slice_in_dim(polar_first, band * band_rows, band_rows, 0)
        - band * source_rows
        + 3
    )
    polar_matrix = stencil_matrix(
        polar_local[:, None] + four_taps,
        lax.dynamic_slice_in_dim(polar_weights, band * band_rows, band_rows, 0),
        source_rows + 6,
    )
    azimuth_local = (
        lax.dynamic_slice_in_dim(azimuth_first, block * block_cols, block_cols, 0)
        - block * source_cols
        + 3
    ) % cols_five
    azimuth_matrix = stencil_matrix(
        azimuth_local[:, None] + four_taps,
        lax.dynamic_slice_in_dim(azimuth_weights, block * block_cols, block_cols, 0),
        source_cols + 6,
    ).T.astype(jnp.bfloat16)

    axial = rows_four / 8.0 * np.cos(sample_angles(rows_four, 1)[0])
    cosine = lax.dynamic_slice_in_dim(
        jnp.asarray(np.cos(axial).astype(np.float32)), band * band_rows, band_rows, 0
    )
    sine = lax.dynamic_slice_in_dim(
        jnp.asarray(np.sin(axial).astype(np.float32)), band * band_rows, band_rows, 0
    )
    whole = polar_matrix[:, 3 : 3 + source_rows]
    edge = jnp.concatenate(
        [
            polar_matrix[:, :3],
            polar_matrix[:, 3 + source_rows :],
            jnp.zeros((band_rows, 10), jnp.float32),
        ],
        axis=1,
    )
    real_row = []
    imag_row = []
    for matrix in (whole, edge):
        in_phase, quadrature = matrix * cosine[:, None], matrix * sine[:, None]
        for sign in (-1.0, 1.0):
            real_row += [in_phase, -sign * quadrature]
            imag_row += [sign * quadrature, in_phase]
    operator4 = jnp.concatenate(
        [jnp.concatenate(real_row, axis=1), jnp.concatenate(imag_row, axis=1)], axis=0
    ).astype(jnp.bfloat16)
    picker = np.zeros((8, source_cols), np.float32)
    for k in range(3):
        picker[k, k] = 1.0
        picker[3 + k, source_cols - 3 + k] = 1.0
    shape4 = (device_count // 2, 2, part, 2)
    halfway4, edges4 = halfway(
        [arrived.reshape(shape4 + arrived.shape[3:]) for arrived in arrived5],
        [edges.reshape(shape4 + edges.shape[3:]) for edges in edges5],
        operator4,
        jnp.asarray(picker, jnp.bfloat16),
    )
    around = [(i, (i + 1) % block_count) for i in range(block_count)]
    from_low = lax.ppermute(edges4, "clu", around)
    from_high = lax.ppermute(edges4, "clu", [(b, a) for a, b in around])
    azimuth_edge = jnp.concatenate(
        [
            jnp.zeros((3, block_cols), jnp.bfloat16),
            azimuth_matrix[:3],
            jnp.zeros((2, block_cols), jnp.bfloat16),
            azimuth_matrix[3 + source_cols :],
            jnp.zeros((5, block_cols), jnp.bfloat16),
        ],
        axis=0,
    )
    factors4 = lax.dynamic_slice(
        jnp.asarray(transverse_factors(rows_four, cols_four)),
        (0, band * band_rows, block * block_cols),
        (4, band_rows, block_cols),
    )
    translated5 = translate(
        arrived5, transfer5, sources5, offsets5, transfer5.shape[2], "translate5"
    )
    level4 = interpolate_phi(
        halfway4,
        from_low,
        from_high,
        azimuth_matrix[3 : 3 + source_cols],
        azimuth_edge,
        factors4,
    )
    translated4 = translate([level4[:, None]], transfer4, sources4, offsets4, 16, "translate4")
    return translated5, translated4


def solution(mesh):
    in_specs = (
        P(("clu", "ang"), None, None, None),
        P(),
        P(),
        P(),
        P(),
        P(),
        P(),
        P(),
        P(),
        P(None, None, "ang", "clu"),
        P(),
        P(),
        P(None, None, "ang", "clu"),
        P(),
        P(),
    )
    out_specs = (P(None, None, "ang", "clu"), P(None, None, "ang", "clu"))
    return jax.shard_map(shards, mesh=mesh, in_specs=in_specs, out_specs=out_specs, check_vma=False)
```

time: 153 us -> 146 us (0.954)
  waiting for transfers between devices: 55.8 us -> 24.5 us
  starting transfers between devices: 10.7 us -> 26.8 us
  local copies, waits for them, and re-layouts: 6.35 us -> 10.2 us
  other arithmetic: 7.48 us -> 9.63 us
  Pallas kernels: 70 us -> 71.9 us
    all_to_all x2, waiting for transfers between devices: 55.8 us -> 22.6 us  [shards(): arrived5.append(lax.all_to_all(windows5, ('clu', 'ang'), 0, 0, tiled=True))]
    ppermute x0 -> x6, starting transfers between devices: none -> 16.7 us  [the longest x2 8.95 us: shards(): high = lax.ppermute(arrived[:, :, :, :3], 'ang', downward)]
    pallas_call x0 -> x2, Pallas kernels: none -> 12.3 us  [the longest x1 6.34 us: halfway(): pl.pallas_call(halfway_kernel, grid=(parents // group,), in_specs=[pl.Blo...]
    pallas_call x3 -> x4, Pallas kernels: 40.9 us -> 30.9 us  [aggregate(): pl.pallas_call(body, grid=(parents // group, chunks), in_specs=[pl.BlockS...]
    dynamic_slice x0 -> x3, local copies, waits for them, and re-layouts: none -> 3.17 us  [the longest x1 1.66 us: shards(): lax.dynamic_slice(jnp.asarray(transverse_factors(rows_four, cols_four)),...]
    concatenate x0 -> x2, other arithmetic: none -> 2.07 us  [the longest x1 1.44 us: shards(): edges5.append(jnp.concatenate([low, high, fill], axis=3))]
    reduce_sum x2, other arithmetic: 2.36 us -> 0.45 us  [stencil_matrix(): return jnp.sum(weights.astype(jnp.float32)[:, :, None] * matches, axis=1)]
    ppermute x0 -> x6, waiting for transfers between devices: none -> 1.87 us  [the longest x2 1.79 us: shards(): high = lax.ppermute(arrived[:, :, :, :3], 'ang', downward)]
  transfers between devices with their start and end apart: 2 -> 8, of which waited for: 2 -> 4; matrix products, arithmetic and copies ran while one was open for 6% -> 10% of each run, Pallas kernels for 21% -> 23%
where the time goes in v2:
time: 146 us; the launch traced here: 144 us
  Pallas kernels  71.9 us (49%)
  starting transfers between devices  26.8 us (18%)
  waiting for transfers between devices  24.5 us (17%)
  local copies, waits for them, and re-layouts  10.2 us (7%)
  other arithmetic  9.63 us (7%)
    pallas_call x4, Pallas kernels, aggregate(): pl.pallas_call(body, grid=(parents // group, chunks), in_specs=[pl.BlockS...  30.9 us
    pallas_call x2, Pallas kernels, translate(): pl.pallas_call(body, grid_spec=pltpu.PrefetchScalarGridSpec(num_scalar_pr...  28.6 us
    all_to_all x2, waiting for transfers between devices, shards(): arrived5.append(lax.all_to_all(windows5, ('clu', 'ang'), 0, 0, tiled=True))  22.6 us
    all_to_all x2, starting transfers between devices, shards(): arrived5.append(lax.all_to_all(windows5, ('clu', 'ang'), 0, 0, tiled=True))  10 us
    ppermute x2, starting transfers between devices, shards(): high = lax.ppermute(arrived[:, :, :, :3], 'ang', downward)  8.95 us
    pallas_call x1, Pallas kernels, halfway(): pl.pallas_call(halfway_kernel, grid=(parents // group,), in_specs=[pl.Blo...  6.34 us
    pallas_call x1, Pallas kernels, interpolate_phi(): pl.pallas_call(phi_kernel, grid=(parents // group,), in_specs=[pl.BlockSp...  6.01 us
    ppermute x2, starting transfers between devices, shards(): low = lax.ppermute(arrived[:, :, :, source_rows - 3:], 'ang', upward)  3.98 us
  transfers between devices with their start and end apart: 8, of which 4 were waited for; matrix products, arithmetic and copies ran while one was open for 10% of the time, Pallas kernels for 23%

profile of v2, /device:TPU:4, one launch (start us, length us, event | category | flops | bytes accessed | tf_op | source)
XLA Modules:
  0.0 143.9 jit_solution(18299783173496218031)
XLA Ops:
  1.4 0.8 copy.54
  2.2 1.0 fusion.2
  3.2 0.8 pad_maximum_fusion
  4.1 8.0 %level6.3 = bf16[16,2,128,256]{3,2,1,0:T(8,128)(2,1)} custom-call(bf16[32,2,4,2,64,128]{5,4,3,2,1,0:T(8,128)(2,1)} %bitcast.27, bf16[1,256,256]{2,1,0:T(8,128)(2,1)} %bitcast.36, bf16[128,256]{1,0:T(8,128)(2,1)} %refs_2_.6, f32[4,128,256]{2,1,0:T(8,128)} %constant.80.clone.refs_3_), custom_call_target="tpu_custom_call" | custom-call | flops 2147483648 | bytes 6815744 | tf_op jit(solution)/shard_map/level6/pallas_call | solution.py:150
  12.1 7.4 %level5.3 = bf16[4,8,2,2,32,128]{5,4,3,2,1,0:T(8,128)(2,1)} custom-call(bf16[2,2,4,2,128,256]{5,4,3,2,1,0:T(8,128)(2,1)} %bitcast.35, bf16[2,256,512]{2,1,0:T(8,128)(2,1)} %bitcast.42, bf16[256,512]{1,0:T(8,128)(2,1)} %refs_2_.7, f32[4,256,512]{2,1,0:T(8,128)} %constant.81.clone.refs_3_), custom_call_target="tpu_custom_call" | custom-call | flops 2147483648 | bytes 5242880 | tf_op jit(solution)/shard_map/level5/pallas_call | solution.py:150
  19.5 6.1 %all-to-all-start.1 = ((bf16[32,2,2,32,128]{4,3,2,1,0:T(8,128)(2,1)}), bf16[32,2,2,32,128]{4,3,2,1,0:T(8,128)(2,1)S(1)}, u32[]{:S(2)}, u32[]{:S(2)}) async-start(bf16[32,2,2,32,128]{4,3,2,1,0:T(8,128)(2,1)} %bitcast.39), calls=%async_computation.1 | async-start | bytes 2097152 | tf_op jit(solution)/shard_map/all_to_all | solution.py:423
  29.0 8.0 %level6.2 = bf16[16,2,128,256]{3,2,1,0:T(8,128)(2,1)} custom-call(bf16[32,2,4,2,64,128]{5,4,3,2,1,0:T(8,128)(2,1)} %bitcast.28, bf16[1,256,256]{2,1,0:T(8,128)(2,1)} %bitcast.37, bf16[128,256]{1,0:T(8,128)(2,1)} %refs_2_.6, f32[4,128,256]{2,1,0:T(8,128)} %constant.80.clone.refs_3_), custom_call_target="tpu_custom_call" | custom-call | flops 2147483648 | bytes 6815744 | tf_op jit(solution)/shard_map/level6/pallas_call | solution.py:150
  37.0 7.5 %level5.2 = bf16[4,8,2,2,32,128]{5,4,3,2,1,0:T(8,128)(2,1)} custom-call(bf16[2,2,4,2,128,256]{5,4,3,2,1,0:T(8,128)(2,1)} %bitcast.34, bf16[2,256,512]{2,1,0:T(8,128)(2,1)} %bitcast.43, bf16[256,512]{1,0:T(8,128)(2,1)} %refs_2_.7, f32[4,256,512]{2,1,0:T(8,128)} %constant.81.clone.refs_3_), custom_call_target="tpu_custom_call" | custom-call | flops 2147483648 | bytes 5242880 | tf_op jit(solution)/shard_map/level5/pallas_call | solution.py:150
  44.6 7.0 %all-to-all-done.1.refs_5_ = bf16[32,2,2,32,128]{4,3,2,1,0:T(8,128)(2,1)S(1)} async-done(((bf16[32,2,2,32,128]{4,3,2,1,0:T(8,128)(2,1)}), bf16[32,2,2,32,128]{4,3,2,1,0:T(8,128)(2,1)S(1)}, u32[]{:S(2)}, u32[]{:S(2)}) %all-to-all-start.1) | async-done | bytes 1048608 | tf_op jit(solution)/shard_map/all_to_all | solution.py:423
  51.6 3.9 %all-to-all-start = ((bf16[32,2,2,32,128]{4,3,2,1,0:T(8,128)(2,1)}), bf16[32,2,2,32,128]{4,3,2,1,0:T(8,128)(2,1)S(1)}, u32[]{:S(2)}, u32[]{:S(2)}) async-start(bf16[32,2,2,32,128]{4,3,2,1,0:T(8,128)(2,1)} %bitcast.38), calls=%async_computation | async-start | bytes 2097152 | tf_op jit(solution)/shard_map/all_to_all | solution.py:423
  59.3 2.1 %collective-permute-start.2 = (bf16[32,2,2,3,128]{4,3,2,1,0:T(4,128)(2,1)S(1)}, bf16[32,2,2,3,128]{4,3,2,1,0:T(4,128)(2,1)S(1)}, u32[]{:S(2)}, u32[]{:S(2)}) collective-permute-start(bf16[32,2,2,3,128]{4,3,2,1,0:T(4,128)(2,1)S(1)} %get-tuple-element.8), channel_id=1, source_target_pairs={{0,1},{1,2},{2,3},{3,4},{4,5},{5,6},{6,7},{8,9},{9,10},{10,11},{11... | collective-permute-start | bytes 294920 | tf_op jit(solution)/shard_map/ppermute | solution.py:429
  61.4 4.4 %collective-permute-start.3 = (bf16[32,2,2,3,128]{4,3,2,1,0:T(4,128)(2,1)S(1)}, bf16[32,2,2,3,128]{4,3,2,1,0:T(4,128)(2,1)S(1)}, u32[]{:S(2)}, u32[]{:S(2)}) collective-permute-start(bf16[32,2,2,3,128]{4,3,2,1,0:T(4,128)(2,1)S(1)} %get-tuple-element.9), channel_id=1, source_target_pairs={{1,0},{2,1},{3,2},{4,3},{5,4},{6,5},{7,6},{9,8},{10,9},{11,10},{12... | collective-permute-start | bytes 294920 | tf_op jit(solution)/shard_map/ppermute | solution.py:430
  65.8 15.7 %all-to-all-done.refs_4_ = bf16[32,2,2,32,128]{4,3,2,1,0:T(8,128)(2,1)S(1)} async-done(((bf16[32,2,2,32,128]{4,3,2,1,0:T(8,128)(2,1)}), bf16[32,2,2,32,128]{4,3,2,1,0:T(8,128)(2,1)S(1)}, u32[]{:S(2)}, u32[]{:S(2)}) %all-to-all-start) | async-done | bytes 1048608 | tf_op jit(solution)/shard_map/all_to_all | solution.py:423
  81.6 1.9 %collective-permute-start = (bf16[32,2,2,3,128]{4,3,2,1,0:T(4,128)(2,1)S(1)}, bf16[32,2,2,3,128]{4,3,2,1,0:T(4,128)(2,1)S(1)}, u32[]{:S(2)}, u32[]{:S(2)}) collective-permute-start(bf16[32,2,2,3,128]{4,3,2,1,0:T(4,128)(2,1)S(1)} %get-tuple-element.10), channel_id=1, source_target_pairs={{0,1},{1,2},{2,3},{3,4},{4,5},{5,6},{6,7},{8,9},{9,10},{10,11},{11... | collective-permute-start | bytes 294920 | tf_op jit(solution)/shard_map/ppermute | solution.py:429
  83.5 4.5 %collective-permute-start.1 = (bf16[32,2,2,3,128]{4,3,2,1,0:T(4,128)(2,1)S(1)}, bf16[32,2,2,3,128]{4,3,2,1,0:T(4,128)(2,1)S(1)}, u32[]{:S(2)}, u32[]{:S(2)}) collective-permute-start(bf16[32,2,2,3,128]{4,3,2,1,0:T(4,128)(2,1)S(1)} %get-tuple-element.11), channel_id=1, source_target_pairs={{1,0},{2,1},{3,2},{4,3},{5,4},{6,5},{7,6},{9,8},{10,9},{11,10},{12... | collective-permute-start | bytes 294920 | tf_op jit(solution)/shard_map/ppermute | solution.py:430
  88.7 1.8 %collective-permute-done.1 = bf16[32,2,2,3,128]{4,3,2,1,0:T(4,128)(2,1)S(1)} collective-permute-done((bf16[32,2,2,3,128]{4,3,2,1,0:T(4,128)(2,1)S(1)}, bf16[32,2,2,3,128]{4,3,2,1,0:T(4,128)(2,1)S(1)}, u32[]{:S(2)}, u32[]{:S(2)}) %collective-permute-start.1) | collective-permute-done | bytes 98336 | tf_op jit(solution)/shard_map/ppermute | solution.py:430
  90.5 1.4 %maximum_maximum_fusion.1 = (bf16[32,2,2,16,128]{4,3,2,1,0:T(8,128)(2,1)}, bf16[32,2,2,16,128]{4,3,2,1,0:T(8,128)(2,1)}) fusion(bf16[32,2,2,3,128]{4,3,2,1,0:T(4,128)(2,1)S(1)} %collective-permute-done.3, bf16[32,2,2,3,128]{4,3,2,1,0:T(4,128)(2,1)S(1)} %collective-permute-done.2, bf16[16]{0:T(256)(128)(2,1)S(1)} %pad.5.clone, ...), kind=kLoop, calls=%fused_computation.4 | loop fusion | flops 2883584 | bytes 1441824 | tf_op jit(solution)/shard_map/concatenate | solution.py:432
  92.0 6.3 %halfway4.1 = (bf16[16,512,128]{2,1,0:T(8,128)(2,1)}, bf16[16,8,512]{2,1,0:T(8,128)(2,1)}) custom-call(bf16[128,192]{1,0:T(8,128)(2,1)} %pad_maximum_fusion.4.m_ref, bf16[8,128]{1,0:T(8,128)(2,1)} %constant.84.clone.e_ref, bf16[16,2,2,2,32,128]{5,4,3,2,1,0:T(8,128)(2,1)} %bitcast.30, bf16[16,2,2,2,32,128]{5,4,3,2,1,0:T(8,128)(2,1)} %bitcast.29, ...), custom_call_target="tpu_custom_call" | custom-call | flops 402653184 | bytes 4194304 | tf_op jit(solution)/shard_map/halfway4/pallas_call | solution.py:199
  98.8 3.3 %collective-permute-start.5 = (bf16[16,8,512]{2,1,0:T(8,128)(2,1)}, bf16[16,8,512]{2,1,0:T(8,128)(2,1)S(1)}, u32[]{:S(2)}, u32[]{:S(2)}) collective-permute-start(bf16[16,8,512]{2,1,0:T(8,128)(2,1)} %get-tuple-element.5), channel_id=1, source_target_pairs={{8,0},{16,8},{24,16},{0,24},{9,1},{17,9},{25,17},{1,25},{10,2},{18... | collective-permute-start | bytes 393224 | tf_op jit(solution)/shard_map/ppermute | solution.py:495
  105.6 1.2 concatenate.52.e_ref
  106.9 1.7 %constant_dynamic-slice_fusion.t_ref = f32[4,64,256]{2,1,0:T(8,128)} fusion(f32[4,512,1024]{2,1,0:T(8,128)} %constant.85.clone, s32[]{:T(128)S(6)} %select_n.29, s32[]{:T(128)S(6)} %select_n.30), kind=kLoop, calls=%fused_computation.49 | loop fusion | bytes 524296 | tf_op jit(solution)/shard_map/dynamic_slice | solution.py:506
  108.5 18.0 %translate5.1 = bf16[128,2,32,128]{3,2,1,0:T(8,128)(2,1)} custom-call(s32[2048]{0:T(1024)} %reshape.111.refs_0_, s32[2048]{0:T(1024)} %reshape.112.refs_1_, s32[128]{0:T(128)} %get-tuple-element.33.refs_2_, bf16[316,2,32,128]{3,2,1,0:T(8,128)(2,1)} %refs_3_.6, bf16[32,2,2,32,128]{4,3,2,1,0:T(8,128)(2,1)} %copy-done.1, bf16[32,2,2,32,128]{4,3,2,1,0:T(8,128)(2,1)} %copy-done), custom_call_target="tpu_custom_call" | custom-call | flops 67108864 | bytes 9371648 | tf_op jit(solution)/shard_map/translate5/pallas_call | solution.py:332
  127.2 6.0 %level4.1 = bf16[16,2,64,256]{3,2,1,0:T(8,128)(2,1)} custom-call(bf16[16,512,128]{2,1,0:T(8,128)(2,1)} %get-tuple-element.4.h_ref, bf16[16,8,512]{2,1,0:T(8,128)(2,1)} %copy-done.2, bf16[16,8,512]{2,1,0:T(8,128)(2,1)} %copy-done.3, bf16[128,256]{1,0:T(8,128)(2,1)} %slice.47.b_ref, bf16[16,256]{1,0:T(8,128)(2,1)} %concatenate.52.e_ref, ...), custom_call_target="tpu_custom_call" | custom-call | flops 603979776 | bytes 4194304 | tf_op jit(solution)/shard_map/level4/pallas_call | solution.py:248
  133.2 10.6 %translate4.1 = bf16[16,2,64,256]{3,2,1,0:T(8,128)(2,1)} custom-call(s32[256]{0:T(256)} %reshape.118.refs_0_, s32[256]{0:T(256)} %reshape.119.refs_1_, s32[16]{0:T(128)} %get-tuple-element.31.refs_2_, bf16[316,2,64,256]{3,2,1,0:T(8,128)(2,1)} %refs_3_.7, bf16[16,1,2,64,256]{4,3,2,1,0:T(8,128)(2,1)} %bitcast.31), custom_call_target="tpu_custom_call" | custom-call | flops 33554432 | bytes 22806528 | tf_op jit(solution)/shard_map/translate4/pallas_call | solution.py:332
  (68 shorter events, 13.5 us)
Async XLA Ops:
  19.5 32.1 %all-to-all-start.1 = ((bf16[32,2,2,32,128]{4,3,2,1,0:T(8,128)(2,1)}), bf16[32,2,2,32,128]{4,3,2,1,0:T(8,128)(2,1)S(1)}, u32[]{:S(2)}, u32[]{:S(2)}) async-start(bf16[32,2,2,32,128]{4,3,2,1,0:T(8,128)(2,1)} %bitcast.39), calls=%async_computation.1 | async-start | bytes 2097152 | tf_op jit(solution)/shard_map/all_to_all | solution.py:423
  37.0 21.0 %copy-start.4 = (s32[16,16]{1,0:T(8,128)S(1)}, s32[16,16]{1,0:T(8,128)}, u32[]{:S(2)}) copy-start(s32[16,16]{1,0:T(8,128)} %param.40) | copy-start | bytes 3076
  37.0 21.7 %copy-start.5 = (s32[16,16]{1,0:T(8,128)S(1)}, s32[16,16]{1,0:T(8,128)}, u32[]{:S(2)}) copy-start(s32[16,16]{1,0:T(8,128)} %param.41) | copy-start | bytes 3076
  37.0 21.7 %copy-start.6 = (s32[128,16]{0,1:T(8,128)S(1)}, s32[128,16]{0,1:T(8,128)}, u32[]{:S(2)}) copy-start(s32[128,16]{0,1:T(8,128)} %param.37) | copy-start | bytes 24580
  37.0 22.2 %copy-start.7 = (s32[128,16]{0,1:T(8,128)S(1)}, s32[128,16]{0,1:T(8,128)}, u32[]{:S(2)}) copy-start(s32[128,16]{0,1:T(8,128)} %param.38) | copy-start | bytes 24580
  51.6 40.4 %copy-start = (bf16[32,2,2,32,128]{4,3,2,1,0:T(8,128)(2,1)}, bf16[32,2,2,32,128]{4,3,2,1,0:T(8,128)(2,1)S(1)}, u32[]{:S(2)}) copy-start(bf16[32,2,2,32,128]{4,3,2,1,0:T(8,128)(2,1)S(1)} %all-to-all-done.1.refs_5_) | copy-start | bytes 3145732
  51.6 29.9 %all-to-all-start = ((bf16[32,2,2,32,128]{4,3,2,1,0:T(8,128)(2,1)}), bf16[32,2,2,32,128]{4,3,2,1,0:T(8,128)(2,1)S(1)}, u32[]{:S(2)}, u32[]{:S(2)}) async-start(bf16[32,2,2,32,128]{4,3,2,1,0:T(8,128)(2,1)} %bitcast.38), calls=%async_computation | async-start | bytes 2097152 | tf_op jit(solution)/shard_map/all_to_all | solution.py:423
  59.3 29.4 %collective-permute-start.2 = (bf16[32,2,2,3,128]{4,3,2,1,0:T(4,128)(2,1)S(1)}, bf16[32,2,2,3,128]{4,3,2,1,0:T(4,128)(2,1)S(1)}, u32[]{:S(2)}, u32[]{:S(2)}) collective-permute-start(bf16[32,2,2,3,128]{4,3,2,1,0:T(4,128)(2,1)S(1)} %get-tuple-element.8), channel_id=1, source_target_pairs={{0,1},{1,2},{2,3},{3,4},{4,5},{5,6},{6,7},{8,9},{9,10},{10,11},{11... | collective-permute-start | bytes 294920 | tf_op jit(solution)/shard_map/ppermute | solution.py:429
  61.4 27.3 %collective-permute-start.3 = (bf16[32,2,2,3,128]{4,3,2,1,0:T(4,128)(2,1)S(1)}, bf16[32,2,2,3,128]{4,3,2,1,0:T(4,128)(2,1)S(1)}, u32[]{:S(2)}, u32[]{:S(2)}) collective-permute-start(bf16[32,2,2,3,128]{4,3,2,1,0:T(4,128)(2,1)S(1)} %get-tuple-element.9), channel_id=1, source_target_pairs={{1,0},{2,1},{3,2},{4,3},{5,4},{6,5},{7,6},{9,8},{10,9},{11,10},{12... | collective-permute-start | bytes 294920 | tf_op jit(solution)/shard_map/ppermute | solution.py:430
  81.4 10.5 %copy-start.1 = (bf16[32,2,2,32,128]{4,3,2,1,0:T(8,128)(2,1)}, bf16[32,2,2,32,128]{4,3,2,1,0:T(8,128)(2,1)S(1)}, u32[]{:S(2)}) copy-start(bf16[32,2,2,32,128]{4,3,2,1,0:T(8,128)(2,1)S(1)} %all-to-all-done.refs_4_) | copy-start | bytes 3145732
  81.6 7.2 %collective-permute-start = (bf16[32,2,2,3,128]{4,3,2,1,0:T(4,128)(2,1)S(1)}, bf16[32,2,2,3,128]{4,3,2,1,0:T(4,128)(2,1)S(1)}, u32[]{:S(2)}, u32[]{:S(2)}) collective-permute-start(bf16[32,2,2,3,128]{4,3,2,1,0:T(4,128)(2,1)S(1)} %get-tuple-element.10), channel_id=1, source_target_pairs={{0,1},{1,2},{2,3},{3,4},{4,5},{5,6},{6,7},{8,9},{9,10},{10,11},{11... | collective-permute-start | bytes 294920 | tf_op jit(solution)/shard_map/ppermute | solution.py:429
  83.5 7.0 %collective-permute-start.1 = (bf16[32,2,2,3,128]{4,3,2,1,0:T(4,128)(2,1)S(1)}, bf16[32,2,2,3,128]{4,3,2,1,0:T(4,128)(2,1)S(1)}, u32[]{:S(2)}, u32[]{:S(2)}) collective-permute-start(bf16[32,2,2,3,128]{4,3,2,1,0:T(4,128)(2,1)S(1)} %get-tuple-element.11), channel_id=1, source_target_pairs={{1,0},{2,1},{3,2},{4,3},{5,4},{6,5},{7,6},{9,8},{10,9},{11,10},{12... | collective-permute-start | bytes 294920 | tf_op jit(solution)/shard_map/ppermute | solution.py:430
  98.3 28.2 %collective-permute-start.4 = (bf16[16,8,512]{2,1,0:T(8,128)(2,1)}, bf16[16,8,512]{2,1,0:T(8,128)(2,1)S(1)}, u32[]{:S(2)}, u32[]{:S(2)}) collective-permute-start(bf16[16,8,512]{2,1,0:T(8,128)(2,1)} %get-tuple-element.5), channel_id=1, source_target_pairs={{0,8},{8,16},{16,24},{24,0},{1,9},{9,17},{17,25},{25,1},{2,10},{10... | collective-permute-start | bytes 393224 | tf_op jit(solution)/shard_map/ppermute | solution.py:494
  98.8 27.7 %collective-permute-start.5 = (bf16[16,8,512]{2,1,0:T(8,128)(2,1)}, bf16[16,8,512]{2,1,0:T(8,128)(2,1)S(1)}, u32[]{:S(2)}, u32[]{:S(2)}) collective-permute-start(bf16[16,8,512]{2,1,0:T(8,128)(2,1)} %get-tuple-element.5), channel_id=1, source_target_pairs={{8,0},{16,8},{24,16},{0,24},{9,1},{17,9},{25,17},{1,25},{10,2},{18... | collective-permute-start | bytes 393224 | tf_op jit(solution)/shard_map/ppermute | solution.py:495
  126.5 0.7 copy-start.2
  126.5 0.7 copy-start.3

commit v3 on v2

--- a/solution.py
+++ b/solution.py
@@ -9,7 +9,6 @@
 from jax.sharding import PartitionSpec as P
 
 VMEM_LIMIT = 58 * 1024 * 1024
-REGROUPS = 2
 
 
 def sample_angles(rows, cols):
@@ -72,115 +71,155 @@
     return real.astype(jnp.bfloat16), imag.astype(jnp.bfloat16)
 
 
-def aggregate_kernel(pairs, width, split, x_ref, m_ref, b_ref, t_ref, o_ref):
-    parents = x_ref.shape[0]
-    rows2, cols = x_ref.shape[3] * x_ref.shape[4], x_ref.shape[5]
-    chunk = t_ref.shape[1]
-    steps = b_ref.shape[1] // width
-
-    def one_parent(p):
-        halves = []
-        for child in range(4):
-            stacked = [x_ref[p, s, child].reshape(rows2, cols) for s in range(pairs)]
-            halves.append(jnp.concatenate(stacked, axis=0))
-        joined = jnp.concatenate(halves, axis=1)
-        h = jnp.dot(m_ref[0], joined, preferred_element_type=jnp.float32)
+def siblings(block, child, pairs):
+    rows2, cols = block.shape[-3] * block.shape[-2], block.shape[-1]
+    stacked = [block[4 * s + child].reshape(rows2, cols) for s in range(pairs)]
+    return jnp.concatenate(stacked, axis=0)
+
+
+def produce_kernel(
+    clu, ang, x_ref, m6, b6, t6, m5, b5, t5, arrived, level6, windows, send_sem, recv_sem, own_sem
+):
+    step = pl.program_id(0)
+    steps = pl.num_programs(0)
+    devices = clu * ang
+    me = lax.axis_index("clu") * ang + lax.axis_index("ang")
+
+    @pl.when(step == 0)
+    def _():
+        barrier = pltpu.get_barrier_semaphore()
+
+        @pl.loop(1, devices)
+        def _(k):
+            other = lax.rem(me + k, devices)
+            pl.semaphore_signal(
+                barrier,
+                inc=1,
+                device_id=(other // ang, lax.rem(other, ang)),
+                device_id_type=pl.DeviceIdType.MESH,
+            )
+
+        pl.semaphore_wait(barrier, devices - 1)
+
+    @pl.loop(0, 8, unroll=2)
+    def _(p):
+        cols = x_ref.shape[4]
+        joined = jnp.concatenate([siblings(x_ref.at[p], o, 2) for o in range(4)], axis=1)
+        h = jnp.dot(m6[...], joined, preferred_element_type=jnp.float32)
         sums = sign_sums(h, cols)
-
-        def columns(j, start):
-            cut = pl.ds(start, width)
-            y = jnp.dot(sums, b_ref[:, cut], preferred_element_type=jnp.float32)
-            both = apply_factors(y, chunk, [t_ref[k, :, cut] for k in range(4)])
+        y = jnp.dot(sums, b6[...], preferred_element_type=jnp.float32)
+        both = apply_factors(y, t6.shape[1], [t6[k] for k in range(4)])
+        for c in range(2):
+            level6[p, c] = both[c]
+
+    cols = level6.shape[3]
+    chunks, chunk2 = m5.shape[:2]
+    chunk = chunk2 // 2
+    band_rows, block_cols = windows.shape[2], windows.shape[3]
+    bands = chunk // band_rows
+    width = min(256, b5.shape[1])
+
+    @pl.loop(0, chunks)
+    def _(u):
+        joined = jnp.concatenate([siblings(level6, o, 2) for o in range(4)], axis=1)
+        h = jnp.dot(m5[u], joined, preferred_element_type=jnp.float32)
+        sums = sign_sums(h, cols)
+        for j in range(b5.shape[1] // width):
+            cut = slice(j * width, (j + 1) * width)
+            y = jnp.dot(sums, b5[:, cut], preferred_element_type=jnp.float32)
+            rows = pl.ds(pl.multiple_of(u * chunk, chunk), chunk)
+            both = apply_factors(y, chunk, [t5[k, rows, cut] for k in range(4)])
             for c in range(2):
-                if split:
-                    band_rows, block_cols = o_ref.shape[4], o_ref.shape[5]
-                    for q in range(width // block_cols):
-                        for band in range(chunk // band_rows):
-                            o_ref[j * (width // block_cols) + q, band, p, c] = both[c][
-                                band * band_rows : (band + 1) * band_rows,
-                                q * block_cols : (q + 1) * block_cols,
-                            ]
-                else:
-                    o_ref[p, c, :, cut] = both[c]
-
-        if steps == 1:
-            columns(0, 0)
-        else:
-
-            @pl.loop(0, steps)
-            def _(j):
-                columns(j, pl.multiple_of(j * width, width))
-
-    if parents == 1:
-        one_parent(0)
-    else:
-
-        @pl.loop(0, parents, unroll=2)
-        def _(p):
-            one_parent(p)
-
-
-def aggregate(children, operator, azimuth, factors, first, parents, group, split, name):
-    _, pairs, _, _, taps, cols = children.shape
-    chunks, chunk2, depth = operator.shape
-    chunk = chunk2 // 2
-    rows, out_cols = factors.shape[1], factors.shape[2]
-    width = min(256, out_cols)
-    if split is None:
-        out_shape = jax.ShapeDtypeStruct((parents, 2, rows, out_cols), jnp.bfloat16)
-        out_spec = pl.BlockSpec((group, 2, chunk, out_cols), lambda p, u: (p, 0, u, 0))
-    else:
-        blocks, bands = split
-        band_rows, block_cols = rows // bands, out_cols // blocks
-        width = max(width, block_cols)
-        out_shape = jax.ShapeDtypeStruct(
-            (blocks, bands, parents, 2, band_rows, block_cols), jnp.bfloat16
+                for q in range(width // block_cols):
+                    for band in range(bands):
+                        target = (j * (width // block_cols) + q) * ang + u * bands + band
+                        windows[step * devices + target, c] = both[c][
+                            band * band_rows : (band + 1) * band_rows,
+                            q * block_cols : (q + 1) * block_cols,
+                        ]
+
+    @pl.loop(1, devices)
+    def _(k):
+        other = lax.rem(me + k, devices)
+        pltpu.make_async_remote_copy(
+            src_ref=windows.at[step * devices + other],
+            dst_ref=arrived.at[step * devices + me],
+            send_sem=send_sem,
+            recv_sem=recv_sem,
+            device_id=(other // ang, lax.rem(other, ang)),
+            device_id_type=pl.DeviceIdType.MESH,
+        ).start()
+
+    pltpu.make_async_copy(
+        windows.at[step * devices + me], arrived.at[step * devices + me], own_sem.at[step]
+    ).start()
+
+    @pl.when(step == steps - 1)
+    def _():
+        away = pl.ds(0, 4 * (devices - 1))
+        everything = pltpu.make_async_remote_copy(
+            src_ref=windows.at[away],
+            dst_ref=arrived.at[away],
+            send_sem=send_sem,
+            recv_sem=recv_sem,
+            device_id=(lax.axis_index("clu"), lax.rem(lax.axis_index("ang") + 1, ang)),
+            device_id_type=pl.DeviceIdType.MESH,
         )
-        out_spec = pl.BlockSpec(
-            (blocks, chunk // band_rows, group, 2, band_rows, block_cols),
-            lambda p, u: (0, u, p, 0, 0, 0),
-        )
+        everything.wait_send()
+        everything.wait_recv()
+        for k in range(4):
+            pltpu.make_async_copy(
+                windows.at[k * devices + me], arrived.at[k * devices + me], own_sem.at[k]
+            ).wait()
+
+
+def produce(children, operators, azimuths, factors, clu, ang):
+    parents = children.shape[0] // 64
+    rows, cols = factors[1].shape[1:]
+    window = (2, rows // ang, cols // clu)
+    devices = clu * ang
 
     def body(*refs):
-        aggregate_kernel(pairs, width, split is not None, *refs)
-
-    skip = first // group
-    flops = 2 * parents * chunks * 4 * (chunk2 * depth * cols + chunk2 * cols * out_cols)
-    moved = 2 * parents * (16 * taps * cols + 2 * rows * out_cols) + 4 * factors.size
+        produce_kernel(clu, ang, *refs)
+
+    def whole(array):
+        zeros = (0,) * array.ndim
+        return pl.BlockSpec(array.shape, lambda p: zeros)
+
+    arguments = [operators[0][0], azimuths[0], factors[0], operators[1], azimuths[1], factors[1]]
     return pl.pallas_call(
         body,
-        grid=(parents // group, chunks),
-        in_specs=[
-            pl.BlockSpec((group, pairs, 4, 2, taps, cols), lambda p, u: (p + skip, 0, 0, 0, 0, 0)),
-            pl.BlockSpec((1, chunk2, depth), lambda p, u: (u, 0, 0)),
-            pl.BlockSpec(azimuth.shape, lambda p, u: (0, 0)),
-            pl.BlockSpec((4, chunk, out_cols), lambda p, u: (0, u, 0)),
-        ],
-        out_specs=out_spec,
-        out_shape=out_shape,
-        compiler_params=pltpu.CompilerParams(vmem_limit_bytes=VMEM_LIMIT),
-        cost_estimate=pl.CostEstimate(flops=flops, bytes_accessed=moved, transcendentals=0),
-        name=name,
-    )(children, operator, azimuth, factors)
-
-
-def halfway_kernel(m_ref, e_ref, *refs):
-    *inputs, h_ref, g_ref = refs
-    count = len(inputs) // 2
-    parents, _, held, _, rows, cols = inputs[0].shape
-    edge_rows = inputs[count].shape[4]
+        grid=(parents,),
+        in_specs=[pl.BlockSpec((8, 8) + children.shape[1:], lambda p: (p, 0, 0, 0, 0))]
+        + [whole(array) for array in arguments],
+        out_specs=pl.BlockSpec(memory_space=pl.ANY),
+        out_shape=jax.ShapeDtypeStruct((parents * devices,) + window, jnp.bfloat16),
+        scratch_shapes=[
+            pltpu.VMEM((8, 2) + factors[0].shape[1:], jnp.bfloat16),
+            pltpu.VMEM((parents * devices,) + window, jnp.bfloat16),
+            pltpu.SemaphoreType.DMA,
+            pltpu.SemaphoreType.DMA,
+            pltpu.SemaphoreType.DMA((4,)),
+        ],
+        compiler_params=pltpu.CompilerParams(
+            vmem_limit_bytes=VMEM_LIMIT, collective_id=0, has_side_effects=True
+        ),
+        name="produce",
+    )(children.reshape((-1, 8) + children.shape[1:]), *arguments)
+
+
+def halfway_kernel(m_ref, e_ref, x_ref, edge_ref, h_ref, g_ref):
+    _, parents, _, _, rows, cols = x_ref.shape
+    edge_rows = edge_ref.shape[4]
 
     @pl.loop(0, parents, unroll=2)
     def _(p):
-        siblings = []
-        for c in range(count):
-            for i in range(held):
-                pieces = [inputs[c][p, s, i].reshape(2 * rows, cols) for s in range(2)]
-                pieces += [
-                    inputs[count + c][p, s, i].reshape(2 * edge_rows, cols) for s in range(2)
-                ]
-                siblings.append(jnp.concatenate(pieces, axis=0))
-        joined = jnp.concatenate(siblings, axis=1)
+        family = []
+        for o in range(4):
+            pieces = [x_ref[o, p, s].reshape(2 * rows, cols) for s in range(2)]
+            pieces += [edge_ref[o, p, s].reshape(2 * edge_rows, cols) for s in range(2)]
+            family.append(jnp.concatenate(pieces, axis=0))
+        joined = jnp.concatenate(family, axis=1)
         h = jnp.dot(m_ref[...], joined, preferred_element_type=jnp.float32)
         sums = sign_sums(h, cols)
         h_ref[p] = sums
@@ -190,10 +229,9 @@
         g_ref[p] = edges.astype(jnp.bfloat16)
 
 
-def halfway(mains, edges, operator, picker):
-    count = len(mains)
-    parents, _, held, _, rows, cols = mains[0].shape
-    edge_rows = edges[0].shape[4]
+def halfway(main, edges, operator, picker):
+    _, parents, _, _, rows, cols = main.shape
+    edge_rows = edges.shape[4]
     group = math.gcd(parents, 4)
     out_rows = 4 * operator.shape[0]
     return pl.pallas_call(
@@ -202,10 +240,9 @@
         in_specs=[
             pl.BlockSpec(operator.shape, lambda p: (0, 0)),
             pl.BlockSpec(picker.shape, lambda p: (0, 0)),
-        ]
-        + [pl.BlockSpec((group, 2, held, 2, rows, cols), lambda p: (p, 0, 0, 0, 0, 0))] * count
-        + [pl.BlockSpec((group, 2, held, 2, edge_rows, cols), lambda p: (p, 0, 0, 0, 0, 0))]
-        * count,
+            pl.BlockSpec((4, group, 2, 2, rows, cols), lambda p: (0, p, 0, 0, 0, 0)),
+            pl.BlockSpec((4, group, 2, 2, edge_rows, cols), lambda p: (0, p, 0, 0, 0, 0)),
+        ],
         out_specs=[
             pl.BlockSpec((group, out_rows, cols), lambda p: (p, 0, 0)),
             pl.BlockSpec((group, picker.shape[0], out_rows), lambda p: (p, 0, 0)),
@@ -221,7 +258,7 @@
             transcendentals=0,
         ),
         name="halfway4",
-    )(operator, picker, *mains, *edges)
+    )(operator, picker, main, edges)
 
 
 def phi_kernel(h_ref, low_ref, high_ref, b_ref, e_ref, t_ref, o_ref):
@@ -268,26 +305,28 @@
     )(h, low, high, azimuth, azimuth_edge, factors)
 
 
-def translate_kernel(slots, src, off, cnt, t_ref, *refs):
-    *inputs, o_ref, held = refs
+def translate_kernel(src, off, x_ref, t_ref, o_ref, held):
     targets = o_ref.shape[0]
-    sources = held.shape[0] - 1
-    senders, part = inputs[0].shape[:2]
+    slots = src.shape[1]
+    parts, senders = x_ref.shape[:2]
+    sources = parts * senders
     held[sources] = jnp.zeros(held.shape[1:], held.dtype)
 
     @pl.loop(0, senders)
     def _(s):
-        for c, x_ref in enumerate(inputs):
-            for i in range(part):
-                held[(s * len(inputs) + c) * part + i] = x_ref[s, i]
-
-    def gather(t, live):
+        for c in range(parts):
+            held[s * parts + c] = x_ref[c, s]
+
+    def gather(t, lower, end):
         real = imag = None
-        for first in range(0, live, 4):
+        for first in range(0, end, 4):
             group_real = group_imag = None
-            for j in range(first, min(first + 4, live)):
-                picked = src[t * slots + j]
-                chosen = off[t * slots + j]
+            for j in range(first, min(first + 4, end)):
+                picked = src[t, j]
+                chosen = off[t, j]
+                if j > lower:
+                    picked = jnp.where(picked < 0, sources, picked)
+                    chosen = jnp.maximum(chosen, 0)
                 pr, pi = held[picked, 0], held[picked, 1]
                 fr, fi = t_ref[chosen, 0], t_ref[chosen, 1]
                 term_real = fr * pr - fi * pi
@@ -301,17 +340,19 @@
         o_ref[t, 0] = real.astype(o_ref.dtype)
         o_ref[t, 1] = imag.astype(o_ref.dtype)
 
-    ends = sorted({min(slots, -(-slots * k // 16) * 4) for k in (2, 3)} | {slots})
+    ends = [end for end in (8, 12) if end < slots] + [slots]
 
     @pl.loop(0, targets)
     def _(t):
-        live = cnt[t]
-        lower = -1
+        lower = 0
         for end in ends:
-
-            @pl.when(jnp.logical_and(live > lower, live <= end))
-            def _(end=end):
-                gather(t, end)
+            wanted = src[t, lower] >= 0
+            if end < slots:
+                wanted = jnp.logical_and(wanted, src[t, end] < 0)
+
+            @pl.when(wanted)
+            def _(lower=lower, end=end):
+                gather(t, lower, end)
 
             lower = end
 
@@ -319,28 +360,18 @@
 def translate(patterns, table, sources, displacements, row_chunk, name):
     targets, slots = sources.shape
     displacement_count, _, rows, cols = table.shape
-    senders, part = patterns[0].shape[:2]
-    held_count = senders * part * len(patterns)
-    live = sources >= 0
-    src = jnp.where(live, sources, held_count).reshape(-1)
-    off = jnp.maximum(displacements, 0).reshape(-1)
-    cnt = jnp.sum(live.astype(jnp.int32), axis=1)
-
-    def body(*refs):
-        translate_kernel(slots, *refs)
-
+    parts, senders = patterns.shape[:2]
     return pl.pallas_call(
-        body,
+        translate_kernel,
         grid_spec=pltpu.PrefetchScalarGridSpec(
-            num_scalar_prefetch=3,
+            num_scalar_prefetch=2,
             grid=(rows // row_chunk,),
             in_specs=[
+                pl.BlockSpec((parts, senders, 2, row_chunk, cols), lambda r, *_: (0, 0, 0, r, 0)),
                 pl.BlockSpec((displacement_count, 2, row_chunk, cols), lambda r, *_: (0, 0, r, 0)),
-            ]
-            + [pl.BlockSpec((senders, part, 2, row_chunk, cols), lambda r, *_: (0, 0, 0, r, 0))]
-            * len(patterns),
+            ],
             out_specs=pl.BlockSpec((targets, 2, row_chunk, cols), lambda r, *_: (0, 0, r, 0)),
-            scratch_shapes=[pltpu.VMEM((held_count + 1, 2, row_chunk, cols), jnp.bfloat16)],
+            scratch_shapes=[pltpu.VMEM((parts * senders + 1, 2, row_chunk, cols), jnp.bfloat16)],
         ),
         out_shape=jax.ShapeDtypeStruct((targets, 2, rows, cols), jnp.bfloat16),
         compiler_params=pltpu.CompilerParams(vmem_limit_bytes=VMEM_LIMIT),
@@ -350,7 +381,7 @@
             transcendentals=0,
         ),
         name=name,
-    )(src, off, cnt, table, *patterns)
+    )(sources, displacements, patterns, table)
 
 
 def stencil_matrix(tap_index, weights, column_count):
@@ -391,45 +422,25 @@
     parents6 = patterns7.shape[0] // 8
     parents5 = parents6 // 8
     assert parents5 == 4
-    part = parents5 // REGROUPS
-    operator6 = polar_operator(polar_up7, (-1.0, 1.0), rows_six)
-    operator5 = polar_operator(polar_up6, (-1.0, 1.0), rows_five // 2)
-    children7 = patterns7.reshape((parents6, 2, 4) + patterns7.shape[1:])
-    arrived5 = []
-    for step in range(REGROUPS):
-        level6 = aggregate(
-            children7,
-            operator6,
-            azimuth_up7,
-            transverse_factors(rows_six, cols_six),
-            step * part * 8,
-            part * 8,
-            8,
-            None,
-            "level6",
-        )
-        windows5 = aggregate(
-            level6.reshape((part, 2, 4) + level6.shape[1:]),
-            operator5,
-            azimuth_up6,
-            transverse_factors(rows_five, cols_five),
-            0,
-            part,
-            1,
-            (block_count, band_count),
-            "level5",
-        )
-        windows5 = windows5.reshape((device_count,) + windows5.shape[2:])
-        arrived5.append(lax.all_to_all(windows5, ("clu", "ang"), 0, 0, tiled=True))
+    arrived5 = produce(
+        patterns7,
+        (
+            polar_operator(polar_up7, (-1.0, 1.0), rows_six),
+            polar_operator(polar_up6, (-1.0, 1.0), rows_five // 2),
+        ),
+        (azimuth_up7, azimuth_up6),
+        (transverse_factors(rows_six, cols_six), transverse_factors(rows_five, cols_five)),
+        block_count,
+        band_count,
+    )
+    arrived5 = arrived5.reshape((parents5, device_count) + arrived5.shape[1:])
 
     upward = [(i, i + 1) for i in range(band_count - 1)]
     downward = [(i + 1, i) for i in range(band_count - 1)]
-    edges5 = []
-    for arrived in arrived5:
-        low = lax.ppermute(arrived[:, :, :, source_rows - 3 :], "ang", upward)
-        high = lax.ppermute(arrived[:, :, :, :3], "ang", downward)
-        fill = jnp.zeros(arrived.shape[:3] + (10, source_cols), jnp.bfloat16)
-        edges5.append(jnp.concatenate([low, high, fill], axis=3))
+    low = lax.ppermute(arrived5[:, :, :, source_rows - 3 :], "ang", upward)
+    high = lax.ppermute(arrived5[:, :, :, :3], "ang", downward)
+    fill = jnp.zeros(arrived5.shape[:3] + (10, source_cols), jnp.bfloat16)
+    edges5 = jnp.concatenate([low, high, fill], axis=3)
 
     four_taps = jnp.arange(4, dtype=jnp.int32)[None, :]
     polar_local = (
@@ -483,10 +494,10 @@
     for k in range(3):
         picker[k, k] = 1.0
         picker[3 + k, source_cols - 3 + k] = 1.0
-    shape4 = (device_count // 2, 2, part, 2)
+    shape4 = (parents5, device_count // 2, 2, 2)
     halfway4, edges4 = halfway(
-        [arrived.reshape(shape4 + arrived.shape[3:]) for arrived in arrived5],
-        [edges.reshape(shape4 + edges.shape[3:]) for edges in edges5],
+        arrived5.reshape(shape4 + arrived5.shape[3:]),
+        edges5.reshape(shape4 + edges5.shape[3:]),
         operator4,
         jnp.asarray(picker, jnp.bfloat16),
     )
@@ -519,7 +530,7 @@
         azimuth_edge,
         factors4,
     )
-    translated4 = translate([level4[:, None]], transfer4, sources4, offsets4, 16, "translate4")
+    translated4 = translate(level4[None], transfer4, sources4, offsets4, 16, "translate4")
     return translated5, translated4
 
 

time: 146 us -> 132 us (0.904)
  Pallas kernels: 71.9 us -> 99.8 us
  waiting for transfers between devices: 24.5 us -> 0.01 us
  starting transfers between devices: 26.8 us -> 11.6 us
    pallas_call x6 -> x3, Pallas kernels: 59.5 us -> 87.5 us  [the longest x1 55.9 us: produce(): pl.pallas_call(body, grid=(parents,), in_specs=[pl.BlockSpec((8, 8) + chi...]
    all_to_all x2 -> x0, waiting for transfers between devices: 22.6 us -> none  [shards(): arrived5.append(lax.all_to_all(windows5, ('clu', 'ang'), 0, 0, tiled=True))]
    all_to_all x2 -> x0, starting transfers between devices: 10 us -> none  [shards(): arrived5.append(lax.all_to_all(windows5, ('clu', 'ang'), 0, 0, tiled=True))]
    ppermute x4 -> x2, starting transfers between devices: 12.9 us -> 6.46 us  [the longest x1 4.13 us: shards(): high = lax.ppermute(arrived5[:, :, :, :3], 'ang', downward)]
    ppermute x1, starting transfers between devices: 0.52 us -> 3.37 us  [shards(): from_low = lax.ppermute(edges4, 'clu', around)]
    reshape x4 -> x0, local copies, waits for them, and re-layouts: 2.63 us -> none  [the longest x2 1.34 us: translate(): src = jnp.where(live, sources, held_count).reshape(-1)]
    ppermute x4 -> x2, waiting for transfers between devices: 1.87 us -> 0.01 us  [the longest x1 0.01 us: shards(): high = lax.ppermute(arrived5[:, :, :, :3], 'ang', downward)]
    ppermute x1, starting transfers between devices: 3.31 us -> 1.74 us  [shards(): from_high = lax.ppermute(edges4, 'clu', [(b, a) for a, b in around])]
  transfers between devices with their start and end apart: 8 -> 4, of which waited for: 4 -> 0; matrix products, arithmetic and copies ran while one was open for 10% -> 9% of each run, Pallas kernels for 23% -> 15%
where the time goes in v3:
time: 132 us; the launch traced here: 131 us
  Pallas kernels  99.8 us (76%)
  starting transfers between devices  11.6 us (9%)
  local copies, waits for them, and re-layouts  10.1 us (8%)
  other arithmetic  8.39 us (6%)
    pallas_call x1, Pallas kernels, produce(): pl.pallas_call(body, grid=(parents,), in_specs=[pl.BlockSpec((8, 8) + chi...  55.9 us
    pallas_call x2, Pallas kernels, translate(): pl.pallas_call(translate_kernel, grid_spec=pltpu.PrefetchScalarGridSpec(n...  31.6 us
    pallas_call x1, Pallas kernels, halfway(): pl.pallas_call(halfway_kernel, grid=(parents // group,), in_specs=[pl.Blo...  6.28 us
    pallas_call x1, Pallas kernels, interpolate_phi(): pl.pallas_call(phi_kernel, grid=(parents // group,), in_specs=[pl.BlockSp...  6.02 us
    ppermute x1, starting transfers between devices, shards(): high = lax.ppermute(arrived5[:, :, :, :3], 'ang', downward)  4.13 us
    ppermute x1, starting transfers between devices, shards(): from_low = lax.ppermute(edges4, 'clu', around)  3.37 us
  transfers between devices with their start and end apart: 4, of which 0 were waited for; matrix products, arithmetic and copies ran while one was open for 9% of the time, Pallas kernels for 15%

profile of v3, /device:TPU:4, one launch (start us, length us, event | category | flops | bytes accessed | tf_op | source)
XLA Modules:
  0.0 130.7 jit_solution(10844715941084327068)
XLA Ops:
  0.6 0.7 fusion.6
  1.4 0.8 copy.45
  2.2 1.0 fusion.2
  3.2 0.8 pad_maximum_fusion
  4.1 55.9 %produce.1 = bf16[128,2,32,128]{3,2,1,0:T(8,128)(2,1)} custom-call(bf16[32,8,2,64,128]{4,3,2,1,0:T(8,128)(2,1)} %bitcast.25, bf16[256,256]{1,0:T(8,128)(2,1)} %bitcast.31, bf16[128,256]{1,0:T(8,128)(2,1)} %refs_2_.1, f32[4,128,256]{2,1,0:T(8,128)} %constant.76.clone.refs_3_, bf16[2,256,512]{2,1,0:T(8,128)(2,1)} %bitcast.28, bf16[256,512]{1,0:T(8,128)(2,1)} %refs_5_.1, ...), custom_call_target="tpu_custom_call" | custom-call | tf_op jit(solution)/shard_map/produce/pallas_call | solution.py:190
  60.0 1.4 %fusion.9 = (bf16[4,32,2,3,128]{4,3,2,1,0:T(4,128)(2,1)S(1)}, bf16[4,32,2,3,128]{4,3,2,1,0:T(4,128)(2,1)S(1)}) fusion(bf16[4,32,2,32,128]{4,3,2,1,0:T(8,128)(2,1)} %bitcast.22), kind=kLoop, calls=%fused_computation.42 | loop fusion | bytes 786432 | tf_op jit(solution)/shard_map/slice | solution.py:440
  61.4 2.3 %collective-permute-start = (bf16[4,32,2,3,128]{4,3,2,1,0:T(4,128)(2,1)S(1)}, bf16[4,32,2,3,128]{4,3,2,1,0:T(4,128)(2,1)S(1)}, u32[]{:S(2)}, u32[]{:S(2)}) collective-permute-start(bf16[4,32,2,3,128]{4,3,2,1,0:T(4,128)(2,1)S(1)} %get-tuple-element.8), channel_id=1, source_target_pairs={{0,1},{1,2},{2,3},{3,4},{4,5},{5,6},{6,7},{8,9},{9,10},{10,11},{11... | collective-permute-start | bytes 589832 | tf_op jit(solution)/shard_map/ppermute | solution.py:440
  63.8 4.1 %collective-permute-start.1 = (bf16[4,32,2,3,128]{4,3,2,1,0:T(4,128)(2,1)S(1)}, bf16[4,32,2,3,128]{4,3,2,1,0:T(4,128)(2,1)S(1)}, u32[]{:S(2)}, u32[]{:S(2)}) collective-permute-start(bf16[4,32,2,3,128]{4,3,2,1,0:T(4,128)(2,1)S(1)} %get-tuple-element.9), channel_id=1, source_target_pairs={{1,0},{2,1},{3,2},{4,3},{5,4},{6,5},{7,6},{9,8},{10,9},{11,10},{12... | collective-permute-start | bytes 589832 | tf_op jit(solution)/shard_map/ppermute | solution.py:441
  67.9 0.8 subtract_add_fusion
  68.7 0.7 dynamic-slice_convert_fusion.1
  69.7 0.8 dynamic_slice.24
  70.5 0.8 dynamic_slice.23
  71.9 0.8 and_select_fusion
  74.5 1.4 %maximum_maximum_fusion = bf16[4,32,2,16,128]{4,3,2,1,0:T(8,128)(2,1)} fusion(bf16[4,32,2,3,128]{4,3,2,1,0:T(4,128)(2,1)S(1)} %collective-permute-done.1, bf16[4,32,2,3,128]{4,3,2,1,0:T(4,128)(2,1)S(1)} %collective-permute-done, bf16[16]{0:T(256)(128)(2,1)S(1)} %pad.2.clone), kind=kLoop, calls=%fused_computation | loop fusion | flops 3145728 | bytes 1441824 | tf_op jit(solution)/shard_map/concatenate | solution.py:443
  75.9 6.3 %halfway4.1 = (bf16[16,512,128]{2,1,0:T(8,128)(2,1)}, bf16[16,8,512]{2,1,0:T(8,128)(2,1)}) custom-call(bf16[128,192]{1,0:T(8,128)(2,1)} %pad_maximum_fusion.4.m_ref, bf16[8,128]{1,0:T(8,128)(2,1)} %constant.80.clone.e_ref, bf16[4,16,2,2,32,128]{5,4,3,2,1,0:T(8,128)(2,1)} %bitcast.23, bf16[4,16,2,2,16,128]{5,4,3,2,1,0:T(8,128)(2,1)} %bitcast.27), custom_call_target="tpu_custom_call" | custom-call | flops 402653184 | bytes 4194304 | tf_op jit(solution)/shard_map/halfway4/pallas_call | solution.py:237
  82.2 3.4 %collective-permute-start.2 = (bf16[16,8,512]{2,1,0:T(8,128)(2,1)}, bf16[16,8,512]{2,1,0:T(8,128)(2,1)S(1)}, u32[]{:S(2)}, u32[]{:S(2)}) collective-permute-start(bf16[16,8,512]{2,1,0:T(8,128)(2,1)} %get-tuple-element.5), channel_id=1, source_target_pairs={{0,8},{8,16},{16,24},{24,0},{1,9},{9,17},{17,25},{25,1},{2,10},{10... | collective-permute-start | bytes 393224 | tf_op jit(solution)/shard_map/ppermute | solution.py:505
  85.6 1.7 %collective-permute-start.3 = (bf16[16,8,512]{2,1,0:T(8,128)(2,1)}, bf16[16,8,512]{2,1,0:T(8,128)(2,1)S(1)}, u32[]{:S(2)}, u32[]{:S(2)}) collective-permute-start(bf16[16,8,512]{2,1,0:T(8,128)(2,1)} %get-tuple-element.5), channel_id=1, source_target_pairs={{8,0},{16,8},{24,16},{0,24},{9,1},{17,9},{25,17},{1,25},{10,2},{18... | collective-permute-start | bytes 393224 | tf_op jit(solution)/shard_map/ppermute | solution.py:506
  88.0 0.7 copy.48.src
  88.7 0.7 copy.49.off
  89.4 1.2 concatenate.48.e_ref
  90.7 20.2 %translate5.1 = bf16[128,2,32,128]{3,2,1,0:T(8,128)(2,1)} custom-call(s32[128,16]{1,0:T(8,128)} %copy.48.src, s32[128,16]{1,0:T(8,128)} %copy.49.off, bf16[4,32,2,32,128]{4,3,2,1,0:T(8,128)(2,1)} %bitcast.24, bf16[316,2,32,128]{3,2,1,0:T(8,128)(2,1)} %t_ref.2), custom_call_target="tpu_custom_call" | custom-call | flops 67108864 | bytes 9371648 | tf_op jit(solution)/shard_map/translate5/pallas_call | solution.py:364
  110.9 1.7 %constant_dynamic-slice_fusion.t_ref = f32[4,64,256]{2,1,0:T(8,128)} fusion(f32[4,512,1024]{2,1,0:T(8,128)} %constant.81.clone, s32[]{:T(128)S(6)} %select_n.11, s32[]{:T(128)S(6)} %select_n.20), kind=kLoop, calls=%fused_computation.40 | loop fusion | bytes 524296 | tf_op jit(solution)/shard_map/dynamic_slice | solution.py:517
  113.3 6.0 %level4.1 = bf16[16,2,64,256]{3,2,1,0:T(8,128)(2,1)} custom-call(bf16[16,512,128]{2,1,0:T(8,128)(2,1)} %get-tuple-element.4.h_ref, bf16[16,8,512]{2,1,0:T(8,128)(2,1)} %copy-done, bf16[16,8,512]{2,1,0:T(8,128)(2,1)} %copy-done.1, bf16[128,256]{1,0:T(8,128)(2,1)} %slice.37.b_ref, bf16[16,256]{1,0:T(8,128)(2,1)} %concatenate.48.e_ref, ...), custom_call_target="tpu_custom_call" | custom-call | flops 603979776 | bytes 4194304 | tf_op jit(solution)/shard_map/level4/pallas_call | solution.py:285
  119.3 11.4 %translate4.1 = bf16[16,2,64,256]{3,2,1,0:T(8,128)(2,1)} custom-call(s32[16,16]{1,0:T(8,128)} %src.2, s32[16,16]{1,0:T(8,128)} %off.2, bf16[1,16,2,64,256]{4,3,2,1,0:T(8,128)(2,1)} %bitcast.26, bf16[316,2,64,256]{3,2,1,0:T(8,128)(2,1)} %t_ref.3), custom_call_target="tpu_custom_call" | custom-call | flops 33554432 | bytes 22806528 | tf_op jit(solution)/shard_map/translate4/pallas_call | solution.py:364
  (40 shorter events, 4.1 us)
Async XLA Ops:
  61.4 13.1 %collective-permute-start = (bf16[4,32,2,3,128]{4,3,2,1,0:T(4,128)(2,1)S(1)}, bf16[4,32,2,3,128]{4,3,2,1,0:T(4,128)(2,1)S(1)}, u32[]{:S(2)}, u32[]{:S(2)}) collective-permute-start(bf16[4,32,2,3,128]{4,3,2,1,0:T(4,128)(2,1)S(1)} %get-tuple-element.8), channel_id=1, source_target_pairs={{0,1},{1,2},{2,3},{3,4},{4,5},{5,6},{6,7},{8,9},{9,10},{10,11},{11... | collective-permute-start | bytes 589832 | tf_op jit(solution)/shard_map/ppermute | solution.py:440
  63.8 10.7 %collective-permute-start.1 = (bf16[4,32,2,3,128]{4,3,2,1,0:T(4,128)(2,1)S(1)}, bf16[4,32,2,3,128]{4,3,2,1,0:T(4,128)(2,1)S(1)}, u32[]{:S(2)}, u32[]{:S(2)}) collective-permute-start(bf16[4,32,2,3,128]{4,3,2,1,0:T(4,128)(2,1)S(1)} %get-tuple-element.9), channel_id=1, source_target_pairs={{1,0},{2,1},{3,2},{4,3},{5,4},{6,5},{7,6},{9,8},{10,9},{11,10},{12... | collective-permute-start | bytes 589832 | tf_op jit(solution)/shard_map/ppermute | solution.py:441
  74.5 13.5 %copy-start.2 = (s32[128,16]{0,1:T(8,128)S(1)}, s32[128,16]{0,1:T(8,128)}, u32[]{:S(2)}) copy-start(s32[128,16]{0,1:T(8,128)} %param.35) | copy-start | bytes 24580
  75.9 12.8 %copy-start.3 = (s32[128,16]{0,1:T(8,128)S(1)}, s32[128,16]{0,1:T(8,128)}, u32[]{:S(2)}) copy-start(s32[128,16]{0,1:T(8,128)} %param.36) | copy-start | bytes 24580
  82.2 30.3 %collective-permute-start.2 = (bf16[16,8,512]{2,1,0:T(8,128)(2,1)}, bf16[16,8,512]{2,1,0:T(8,128)(2,1)S(1)}, u32[]{:S(2)}, u32[]{:S(2)}) collective-permute-start(bf16[16,8,512]{2,1,0:T(8,128)(2,1)} %get-tuple-element.5), channel_id=1, source_target_pairs={{0,8},{8,16},{16,24},{24,0},{1,9},{9,17},{17,25},{25,1},{2,10},{10... | collective-permute-start | bytes 393224 | tf_op jit(solution)/shard_map/ppermute | solution.py:505
  85.6 27.0 %collective-permute-start.3 = (bf16[16,8,512]{2,1,0:T(8,128)(2,1)}, bf16[16,8,512]{2,1,0:T(8,128)(2,1)S(1)}, u32[]{:S(2)}, u32[]{:S(2)}) collective-permute-start(bf16[16,8,512]{2,1,0:T(8,128)(2,1)} %get-tuple-element.5), channel_id=1, source_target_pairs={{8,0},{16,8},{24,16},{0,24},{9,1},{17,9},{25,17},{1,25},{10,2},{18... | collective-permute-start | bytes 393224 | tf_op jit(solution)/shard_map/ppermute | solution.py:506
  112.6 0.6 copy-start
  112.6 0.7 copy-start.1

commit v4 on v3

--- a/solution.py
+++ b/solution.py
@@ -208,9 +208,36 @@
     )(children.reshape((-1, 8) + children.shape[1:]), *arguments)
 
 
-def halfway_kernel(m_ref, e_ref, x_ref, edge_ref, h_ref, g_ref):
+def halfway_kernel(place, s_ref, e_ref, x_ref, edge_ref, h_ref, g_ref, m_ref):
     _, parents, _, _, rows, cols = x_ref.shape
     edge_rows = edge_ref.shape[4]
+    band_rows = s_ref.shape[0]
+
+    @pl.when(pl.program_id(0) == 0)
+    def _():
+        stencil = s_ref[...]
+        first = stencil[:, 0:1].astype(jnp.int32) - place[0] * rows
+
+        def matrix(position):
+            total = jnp.zeros(position.shape, jnp.float32)
+            for k in range(4):
+                total = total + jnp.where(position == first + k, stencil[:, 1 + k : 2 + k], 0.0)
+            return total
+
+        inner = lax.broadcasted_iota(jnp.int32, (band_rows, rows), 1)
+        outer = lax.broadcasted_iota(jnp.int32, (band_rows, edge_rows), 1)
+        outer = jnp.where(outer < 3, outer - 3, jnp.where(outer < 6, outer + rows - 3, -100))
+        start = 0
+        for whole in (matrix(inner), matrix(outer)):
+            in_phase = (whole * stencil[:, 5:6]).astype(jnp.bfloat16)
+            quadrature = (whole * stencil[:, 6:7]).astype(jnp.bfloat16)
+            width = whole.shape[1]
+            for left, right in ((in_phase, quadrature), (in_phase, -quadrature)):
+                m_ref[:band_rows, start : start + width] = left
+                m_ref[band_rows:, start : start + width] = -right
+                m_ref[:band_rows, start + width : start + 2 * width] = right
+                m_ref[band_rows:, start + width : start + 2 * width] = left
+                start += 2 * width
 
     @pl.loop(0, parents, unroll=2)
     def _(p):
@@ -229,41 +256,74 @@
         g_ref[p] = edges.astype(jnp.bfloat16)
 
 
-def halfway(main, edges, operator, picker):
+def halfway(main, edges, stencil, picker, place, band_rows):
     _, parents, _, _, rows, cols = main.shape
     edge_rows = edges.shape[4]
     group = math.gcd(parents, 4)
-    out_rows = 4 * operator.shape[0]
+    out_rows = 8 * band_rows
+    depth = 4 * (rows + edge_rows)
     return pl.pallas_call(
         halfway_kernel,
-        grid=(parents // group,),
-        in_specs=[
-            pl.BlockSpec(operator.shape, lambda p: (0, 0)),
-            pl.BlockSpec(picker.shape, lambda p: (0, 0)),
-            pl.BlockSpec((4, group, 2, 2, rows, cols), lambda p: (0, p, 0, 0, 0, 0)),
-            pl.BlockSpec((4, group, 2, 2, edge_rows, cols), lambda p: (0, p, 0, 0, 0, 0)),
-        ],
-        out_specs=[
-            pl.BlockSpec((group, out_rows, cols), lambda p: (p, 0, 0)),
-            pl.BlockSpec((group, picker.shape[0], out_rows), lambda p: (p, 0, 0)),
-        ],
+        grid_spec=pltpu.PrefetchScalarGridSpec(
+            num_scalar_prefetch=1,
+            grid=(parents // group,),
+            in_specs=[
+                pl.BlockSpec((band_rows, stencil.shape[1]), lambda p, at: (at[0], 0)),
+                pl.BlockSpec(picker.shape, lambda p, at: (0, 0)),
+                pl.BlockSpec((4, group, 2, 2, rows, cols), lambda p, at: (0, p, 0, 0, 0, 0)),
+                pl.BlockSpec((4, group, 2, 2, edge_rows, cols), lambda p, at: (0, p, 0, 0, 0, 0)),
+            ],
+            out_specs=[
+                pl.BlockSpec((group, out_rows, cols), lambda p, at: (p, 0, 0)),
+                pl.BlockSpec((group, picker.shape[0], out_rows), lambda p, at: (p, 0, 0)),
+            ],
+            scratch_shapes=[pltpu.VMEM((2 * band_rows, depth), jnp.bfloat16)],
+        ),
         out_shape=[
             jax.ShapeDtypeStruct((parents, out_rows, cols), jnp.bfloat16),
             jax.ShapeDtypeStruct((parents, picker.shape[0], out_rows), jnp.bfloat16),
         ],
         compiler_params=pltpu.CompilerParams(vmem_limit_bytes=VMEM_LIMIT),
         cost_estimate=pl.CostEstimate(
-            flops=2 * parents * operator.size * 4 * cols,
+            flops=2 * parents * out_rows * depth * cols,
             bytes_accessed=4 * parents * out_rows * cols,
             transcendentals=0,
         ),
         name="halfway4",
-    )(operator, picker, main, edges)
-
-
-def phi_kernel(h_ref, low_ref, high_ref, b_ref, e_ref, t_ref, o_ref):
+    )(place, stencil, picker, main, edges)
+
+
+def phi_kernel(circle, place, h_ref, low_ref, high_ref, f_ref, w_ref, t_ref, o_ref, b_ref, e_ref):
     parents = h_ref.shape[0]
     chunk = t_ref.shape[1]
+    cols, out_cols = b_ref.shape
+
+    @pl.when(pl.program_id(0) == 0)
+    def _():
+        first = f_ref[...]
+        weights = w_ref[...].astype(jnp.float32)
+        base = place[1] * cols
+
+        def matrix(position):
+            total = jnp.zeros(position.shape, jnp.float32)
+            for k in range(4):
+                tap = first + k
+                tap = jnp.where(tap >= circle, tap - circle, tap)
+                total = total + jnp.where(position == tap, weights[k : k + 1], 0.0)
+            return total.astype(jnp.bfloat16)
+
+        b_ref[...] = matrix(base + lax.broadcasted_iota(jnp.int32, (cols, out_cols), 0))
+        row = lax.broadcasted_iota(jnp.int32, (16, out_cols), 0)
+        low = base + row - 6
+        low = jnp.where(low < 0, low + circle, low)
+        high = base + cols + row - 8
+        high = jnp.where(high >= circle, high - circle, high)
+        position = jnp.where(
+            jnp.logical_and(row >= 3, row < 6),
+            low,
+            jnp.where(jnp.logical_and(row >= 8, row < 11), high, -100),
+        )
+        e_ref[...] = matrix(position)
 
     @pl.loop(0, parents, unroll=2)
     def _(p):
@@ -277,23 +337,33 @@
             o_ref[p, c] = both[c]
 
 
-def interpolate_phi(h, low, high, azimuth, azimuth_edge, factors):
+def interpolate_phi(h, low, high, first, weights, factors, circle, place, rows, out_cols):
     parents, rows8, cols = h.shape
-    _, rows, out_cols = factors.shape
     group = math.gcd(parents, 4)
-    edge_spec = pl.BlockSpec((group,) + low.shape[1:], lambda p: (p, 0, 0))
+    edge_spec = pl.BlockSpec((group,) + low.shape[1:], lambda p, at: (p, 0, 0))
+
+    def body(*refs):
+        phi_kernel(circle, *refs)
+
     return pl.pallas_call(
-        phi_kernel,
-        grid=(parents // group,),
-        in_specs=[
-            pl.BlockSpec((group, rows8, cols), lambda p: (p, 0, 0)),
-            edge_spec,
-            edge_spec,
-            pl.BlockSpec(azimuth.shape, lambda p: (0, 0)),
-            pl.BlockSpec(azimuth_edge.shape, lambda p: (0, 0)),
-            pl.BlockSpec(factors.shape, lambda p: (0, 0, 0)),
-        ],
-        out_specs=pl.BlockSpec((group, 2, rows, out_cols), lambda p: (p, 0, 0, 0)),
+        body,
+        grid_spec=pltpu.PrefetchScalarGridSpec(
+            num_scalar_prefetch=1,
+            grid=(parents // group,),
+            in_specs=[
+                pl.BlockSpec((group, rows8, cols), lambda p, at: (p, 0, 0)),
+                edge_spec,
+                edge_spec,
+                pl.BlockSpec((1, out_cols), lambda p, at: (0, at[1])),
+                pl.BlockSpec((4, out_cols), lambda p, at: (0, at[1])),
+                pl.BlockSpec((4, rows, out_cols), lambda p, at: (0, at[0], at[1])),
+            ],
+            out_specs=pl.BlockSpec((group, 2, rows, out_cols), lambda p, at: (p, 0, 0, 0)),
+            scratch_shapes=[
+                pltpu.VMEM((cols, out_cols), jnp.bfloat16),
+                pltpu.VMEM((16, out_cols), jnp.bfloat16),
+            ],
+        ),
         out_shape=jax.ShapeDtypeStruct((parents, 2, rows, out_cols), jnp.bfloat16),
         compiler_params=pltpu.CompilerParams(vmem_limit_bytes=VMEM_LIMIT),
         cost_estimate=pl.CostEstimate(
@@ -302,12 +372,12 @@
             transcendentals=0,
         ),
         name="level4",
-    )(h, low, high, azimuth, azimuth_edge, factors)
-
-
-def translate_kernel(src, off, x_ref, t_ref, o_ref, held):
+    )(place, h, low, high, first, weights, factors)
+
+
+def translate_kernel(slot_first, src, off, x_ref, t_ref, o_ref, held):
     targets = o_ref.shape[0]
-    slots = src.shape[1]
+    slots = src.shape[0 if slot_first else 1]
     parts, senders = x_ref.shape[:2]
     sources = parts * senders
     held[sources] = jnp.zeros(held.shape[1:], held.dtype)
@@ -317,16 +387,16 @@
         for c in range(parts):
             held[s * parts + c] = x_ref[c, s]
 
-    def gather(t, lower, end):
+    def read(ref, slot, t):
+        return ref[slot, t] if slot_first else ref[t, slot]
+
+    def gather(t, end):
         real = imag = None
         for first in range(0, end, 4):
             group_real = group_imag = None
             for j in range(first, min(first + 4, end)):
-                picked = src[t, j]
-                chosen = off[t, j]
-                if j > lower:
-                    picked = jnp.where(picked < 0, sources, picked)
-                    chosen = jnp.maximum(chosen, 0)
+                picked = read(src, j, t)
+                chosen = read(off, j, t)
                 pr, pi = held[picked, 0], held[picked, 1]
                 fr, fi = t_ref[chosen, 0], t_ref[chosen, 1]
                 term_real = fr * pr - fi * pi
@@ -346,13 +416,13 @@
     def _(t):
         lower = 0
         for end in ends:
-            wanted = src[t, lower] >= 0
+            wanted = read(src, lower, t) < sources
             if end < slots:
-                wanted = jnp.logical_and(wanted, src[t, end] < 0)
+                wanted = jnp.logical_and(wanted, read(src, end, t) == sources)
 
             @pl.when(wanted)
-            def _(lower=lower, end=end):
-                gather(t, lower, end)
+            def _(end=end):
+                gather(t, end)
 
             lower = end
 
@@ -361,8 +431,17 @@
     targets, slots = sources.shape
     displacement_count, _, rows, cols = table.shape
     parts, senders = patterns.shape[:2]
+    src = jnp.where(sources < 0, parts * senders, sources)
+    off = jnp.maximum(displacements, 0)
+    slot_first = targets > slots
+    if slot_first:
+        src, off = src.T, off.T
+
+    def body(*refs):
+        translate_kernel(slot_first, *refs)
+
     return pl.pallas_call(
-        translate_kernel,
+        body,
         grid_spec=pltpu.PrefetchScalarGridSpec(
             num_scalar_prefetch=2,
             grid=(rows // row_chunk,),
@@ -381,14 +460,7 @@
             transcendentals=0,
         ),
         name=name,
-    )(sources, displacements, patterns, table)
-
-
-def stencil_matrix(tap_index, weights, column_count):
-    matches = (
-        tap_index[:, :, None] == jnp.arange(column_count, dtype=jnp.int32)[None, None, :]
-    ).astype(jnp.float32)
-    return jnp.sum(weights.astype(jnp.float32)[:, :, None] * matches, axis=1)
+    )(src, off, patterns, table)
 
 
 def shards(
@@ -442,54 +514,16 @@
     fill = jnp.zeros(arrived5.shape[:3] + (10, source_cols), jnp.bfloat16)
     edges5 = jnp.concatenate([low, high, fill], axis=3)
 
-    four_taps = jnp.arange(4, dtype=jnp.int32)[None, :]
-    polar_local = (
-        lax.dynamic_slice_in_dim(polar_first, band * band_rows, band_rows, 0)
-        - band * source_rows
-        + 3
-    )
-    polar_matrix = stencil_matrix(
-        polar_local[:, None] + four_taps,
-        lax.dynamic_slice_in_dim(polar_weights, band * band_rows, band_rows, 0),
-        source_rows + 6,
-    )
-    azimuth_local = (
-        lax.dynamic_slice_in_dim(azimuth_first, block * block_cols, block_cols, 0)
-        - block * source_cols
-        + 3
-    ) % cols_five
-    azimuth_matrix = stencil_matrix(
-        azimuth_local[:, None] + four_taps,
-        lax.dynamic_slice_in_dim(azimuth_weights, block * block_cols, block_cols, 0),
-        source_cols + 6,
-    ).T.astype(jnp.bfloat16)
-
     axial = rows_four / 8.0 * np.cos(sample_angles(rows_four, 1)[0])
-    cosine = lax.dynamic_slice_in_dim(
-        jnp.asarray(np.cos(axial).astype(np.float32)), band * band_rows, band_rows, 0
-    )
-    sine = lax.dynamic_slice_in_dim(
-        jnp.asarray(np.sin(axial).astype(np.float32)), band * band_rows, band_rows, 0
-    )
-    whole = polar_matrix[:, 3 : 3 + source_rows]
-    edge = jnp.concatenate(
+    stencil = jnp.concatenate(
         [
-            polar_matrix[:, :3],
-            polar_matrix[:, 3 + source_rows :],
-            jnp.zeros((band_rows, 10), jnp.float32),
+            polar_first.astype(jnp.float32)[:, None],
+            polar_weights.astype(jnp.float32),
+            jnp.asarray(np.stack([np.cos(axial), np.sin(axial), 0 * axial], 1), jnp.float32),
         ],
         axis=1,
     )
-    real_row = []
-    imag_row = []
-    for matrix in (whole, edge):
-        in_phase, quadrature = matrix * cosine[:, None], matrix * sine[:, None]
-        for sign in (-1.0, 1.0):
-            real_row += [in_phase, -sign * quadrature]
-            imag_row += [sign * quadrature, in_phase]
-    operator4 = jnp.concatenate(
-        [jnp.concatenate(real_row, axis=1), jnp.concatenate(imag_row, axis=1)], axis=0
-    ).astype(jnp.bfloat16)
+    place = jnp.stack([band, block]).astype(jnp.int32)
     picker = np.zeros((8, source_cols), np.float32)
     for k in range(3):
         picker[k, k] = 1.0
@@ -498,27 +532,14 @@
     halfway4, edges4 = halfway(
         arrived5.reshape(shape4 + arrived5.shape[3:]),
         edges5.reshape(shape4 + edges5.shape[3:]),
-        operator4,
+        stencil,
         jnp.asarray(picker, jnp.bfloat16),
+        place,
+        band_rows,
     )
     around = [(i, (i + 1) % block_count) for i in range(block_count)]
     from_low = lax.ppermute(edges4, "clu", around)
     from_high = lax.ppermute(edges4, "clu", [(b, a) for a, b in around])
-    azimuth_edge = jnp.concatenate(
-        [
-            jnp.zeros((3, block_cols), jnp.bfloat16),
-            azimuth_matrix[:3],
-            jnp.zeros((2, block_cols), jnp.bfloat16),
-            azimuth_matrix[3 + source_cols :],
-            jnp.zeros((5, block_cols), jnp.bfloat16),
-        ],
-        axis=0,
-    )
-    factors4 = lax.dynamic_slice(
-        jnp.asarray(transverse_factors(rows_four, cols_four)),
-        (0, band * band_rows, block * block_cols),
-        (4, band_rows, block_cols),
-    )
     translated5 = translate(
         arrived5, transfer5, sources5, offsets5, transfer5.shape[2], "translate5"
     )
@@ -526,9 +547,13 @@
         halfway4,
         from_low,
         from_high,
-        azimuth_matrix[3 : 3 + source_cols],
-        azimuth_edge,
-        factors4,
+        azimuth_first[None],
+        azimuth_weights.T,
+        jnp.asarray(transverse_factors(rows_four, cols_four)),
+        cols_five,
+        place,
+        band_rows,
+        block_cols,
     )
     translated4 = translate(level4[None], transfer4, sources4, offsets4, 16, "translate4")
     return translated5, translated4

time: 132 us -> 128 us (0.970)
  local copies, waits for them, and re-layouts: 10.1 us -> 3.82 us
  waiting for transfers between devices: 0.01 us -> 5.06 us
  other arithmetic: 8.39 us -> 5.96 us
    ppermute x1, waiting for transfers between devices: 0.01 us -> 3.87 us  [shards(): from_low = lax.ppermute(edges4, 'clu', around)]
    dynamic_slice x3 -> x0, local copies, waits for them, and re-layouts: 3.19 us -> none  [the longest x1 1.68 us: shards(): lax.dynamic_slice(jnp.asarray(transverse_factors(rows_four, cols_four)),...]
    unnamed x11 -> x18, local copies, waits for them, and re-layouts: 2.22 us -> 0.68 us
    convert_element_type x2, other arithmetic: 1.43 us -> 0.01 us  [the longest x1 0.01 us: shards(): polar_weights.astype(jnp.float32)]
  transfers between devices with their start and end apart: 4 -> 4, of which waited for: 0 -> 2; matrix products, arithmetic and copies ran while one was open for 9% -> 2% of each run, Pallas kernels for 15% -> 15%
where the time goes in v4:
time: 128 us
  Pallas kernels  101 us (79%)
  starting transfers between devices  11.5 us (9%)
  other arithmetic  5.96 us (5%)
  waiting for transfers between devices  5.06 us (4%)
  local copies, waits for them, and re-layouts  3.82 us (3%)
    pallas_call x1, Pallas kernels, produce(): pl.pallas_call(body, grid=(parents,), in_specs=[pl.BlockSpec((8, 8) + chi...  56 us
    pallas_call x2, Pallas kernels, translate(): pl.pallas_call(body, grid_spec=pltpu.PrefetchScalarGridSpec(num_scalar_pr...  30.4 us
    pallas_call x1, Pallas kernels, halfway(): pl.pallas_call(halfway_kernel, grid_spec=pltpu.PrefetchScalarGridSpec(num...  7.39 us
    pallas_call x1, Pallas kernels, interpolate_phi(): pl.pallas_call(body, grid_spec=pltpu.PrefetchScalarGridSpec(num_scalar_pr...  6.77 us
    ppermute x1, starting transfers between devices, shards(): high = lax.ppermute(arrived5[:, :, :, :3], 'ang', downward)  4.23 us
    ppermute x1, waiting for transfers between devices, shards(): from_low = lax.ppermute(edges4, 'clu', around)  3.87 us
    ppermute x1, starting transfers between devices, shards(): from_low = lax.ppermute(edges4, 'clu', around)  3.37 us
  transfers between devices with their start and end apart: 4, of which 2 were waited for; matrix products, arithmetic and copies ran while one was open for 2% of the time, Pallas kernels for 15%

profile of v4, /device:TPU:4, one launch (start us, length us, event | category | flops | bytes accessed | tf_op | source)
XLA Modules:
  0.0 127.7 jit_solution(9319839690542826260)
XLA Ops:
  0.6 0.7 fusion.6
  1.4 0.8 copy.35
  2.2 1.0 fusion.2
  3.2 0.8 pad_maximum_fusion
  4.1 0.0 copy-start.2
  4.1 56.0 %produce.1 = bf16[128,2,32,128]{3,2,1,0:T(8,128)(2,1)} custom-call(bf16[32,8,2,64,128]{4,3,2,1,0:T(8,128)(2,1)} %bitcast.31, bf16[256,256]{1,0:T(8,128)(2,1)} %bitcast.37, bf16[128,256]{1,0:T(8,128)(2,1)} %refs_2_.1, f32[4,128,256]{2,1,0:T(8,128)} %constant.42.clone.refs_3_, bf16[2,256,512]{2,1,0:T(8,128)(2,1)} %bitcast.34, bf16[256,512]{1,0:T(8,128)(2,1)} %refs_5_.1, ...), custom_call_target="tpu_custom_call" | custom-call | tf_op jit(solution)/shard_map/produce/pallas_call | solution.py:190
  60.2 1.4 %fusion.9 = (bf16[4,32,2,3,128]{4,3,2,1,0:T(4,128)(2,1)S(1)}, bf16[4,32,2,3,128]{4,3,2,1,0:T(4,128)(2,1)S(1)}) fusion(bf16[4,32,2,32,128]{4,3,2,1,0:T(8,128)(2,1)} %bitcast.28), kind=kLoop, calls=%fused_computation.26 | loop fusion | bytes 786432 | tf_op jit(solution)/shard_map/slice | solution.py:512
  61.6 2.2 %collective-permute-start = (bf16[4,32,2,3,128]{4,3,2,1,0:T(4,128)(2,1)S(1)}, bf16[4,32,2,3,128]{4,3,2,1,0:T(4,128)(2,1)S(1)}, u32[]{:S(2)}, u32[]{:S(2)}) collective-permute-start(bf16[4,32,2,3,128]{4,3,2,1,0:T(4,128)(2,1)S(1)} %get-tuple-element.6), channel_id=1, source_target_pairs={{0,1},{1,2},{2,3},{3,4},{4,5},{5,6},{6,7},{8,9},{9,10},{10,11},{11... | collective-permute-start | bytes 589832 | tf_op jit(solution)/shard_map/ppermute | solution.py:512
  63.8 4.2 %collective-permute-start.1 = (bf16[4,32,2,3,128]{4,3,2,1,0:T(4,128)(2,1)S(1)}, bf16[4,32,2,3,128]{4,3,2,1,0:T(4,128)(2,1)S(1)}, u32[]{:S(2)}, u32[]{:S(2)}) collective-permute-start(bf16[4,32,2,3,128]{4,3,2,1,0:T(4,128)(2,1)S(1)} %get-tuple-element.7), channel_id=1, source_target_pairs={{1,0},{2,1},{3,2},{4,3},{5,4},{6,5},{7,6},{9,8},{10,9},{11,10},{12... | collective-permute-start | bytes 589832 | tf_op jit(solution)/shard_map/ppermute | solution.py:513
  68.1 0.6 fusion.8
  68.7 0.9 copy.38.s_ref
  69.6 0.1 pad.2.clone
  69.7 19.0 %translate5.1 = bf16[128,2,32,128]{3,2,1,0:T(8,128)(2,1)} custom-call(s32[16,128]{1,0:T(8,128)} %get-tuple-element.18.refs_0_, s32[16,128]{1,0:T(8,128)} %get-tuple-element.19.refs_1_, bf16[4,32,2,32,128]{4,3,2,1,0:T(8,128)(2,1)} %bitcast.29, bf16[316,2,32,128]{3,2,1,0:T(8,128)(2,1)} %refs_3_.3), custom_call_target="tpu_custom_call" | custom-call | flops 67108864 | bytes 9371648 | tf_op jit(solution)/shard_map/translate5/pallas_call | solution.py:443
  88.7 0.7 pad_add_fusion.place.refs_0_
  89.4 1.4 %maximum_maximum_fusion = bf16[4,32,2,16,128]{4,3,2,1,0:T(8,128)(2,1)} fusion(bf16[4,32,2,3,128]{4,3,2,1,0:T(4,128)(2,1)S(1)} %collective-permute-done.1, bf16[4,32,2,3,128]{4,3,2,1,0:T(4,128)(2,1)S(1)} %collective-permute-done, bf16[16]{0:T(256)(128)(2,1)S(1)} %pad.2.clone), kind=kLoop, calls=%fused_computation | loop fusion | flops 3145728 | bytes 1441824 | tf_op jit(solution)/shard_map/concatenate | solution.py:515
  90.8 7.4 %halfway4.1 = (bf16[16,512,128]{2,1,0:T(8,128)(2,1)}, bf16[16,8,512]{2,1,0:T(8,128)(2,1)}) custom-call(s32[2]{0:T(128)} %pad_add_fusion.place.refs_0_, f32[512,8]{1,0:T(8,128)} %copy.38.s_ref, bf16[8,128]{1,0:T(8,128)(2,1)} %constant.45.clone.e_ref, bf16[4,16,2,2,32,128]{5,4,3,2,1,0:T(8,128)(2,1)} %bitcast.30, bf16[4,16,2,2,16,128]{5,4,3,2,1,0:T(8,128)(2,1)} %bitcast.33), custom_call_target="tpu_custom_call" | custom-call | flops 402653184 | bytes 4194304 | tf_op jit(solution)/shard_map/halfway4/pallas_call | solution.py:265
  98.2 3.4 %collective-permute-start.2 = (bf16[16,8,512]{2,1,0:T(8,128)(2,1)}, bf16[16,8,512]{2,1,0:T(8,128)(2,1)S(1)}, u32[]{:S(2)}, u32[]{:S(2)}) collective-permute-start(bf16[16,8,512]{2,1,0:T(8,128)(2,1)} %get-tuple-element.5), channel_id=1, source_target_pairs={{0,8},{8,16},{16,24},{24,0},{1,9},{9,17},{17,25},{25,1},{2,10},{10... | collective-permute-start | bytes 393224 | tf_op jit(solution)/shard_map/ppermute | solution.py:541
  101.5 1.7 %collective-permute-start.3 = (bf16[16,8,512]{2,1,0:T(8,128)(2,1)}, bf16[16,8,512]{2,1,0:T(8,128)(2,1)S(1)}, u32[]{:S(2)}, u32[]{:S(2)}) collective-permute-start(bf16[16,8,512]{2,1,0:T(8,128)(2,1)} %get-tuple-element.5), channel_id=1, source_target_pairs={{8,0},{16,8},{24,16},{0,24},{9,1},{17,9},{25,17},{1,25},{10,2},{18... | collective-permute-start | bytes 393224 | tf_op jit(solution)/shard_map/ppermute | solution.py:542
  103.2 0.6 compare_select_fusion
  103.8 3.9 %collective-permute-done.2.refs_2_ = bf16[16,8,512]{2,1,0:T(8,128)(2,1)S(1)} collective-permute-done((bf16[16,8,512]{2,1,0:T(8,128)(2,1)}, bf16[16,8,512]{2,1,0:T(8,128)(2,1)S(1)}, u32[]{:S(2)}, u32[]{:S(2)}) %collective-permute-start.2) | collective-permute-done | bytes 131104 | tf_op jit(solution)/shard_map/ppermute | solution.py:541
  107.7 1.2 collective-permute-done.3.refs_3_
  108.9 0.6 copy-done.1
  109.6 6.8 %level4.1 = bf16[16,2,64,256]{3,2,1,0:T(8,128)(2,1)} custom-call(s32[2]{0:T(128)} %pad_add_fusion.place.refs_0_, bf16[16,512,128]{2,1,0:T(8,128)(2,1)} %get-tuple-element.4.refs_1_, bf16[16,8,512]{2,1,0:T(8,128)(2,1)} %copy-done, bf16[16,8,512]{2,1,0:T(8,128)(2,1)} %copy-done.1, s32[1,1024]{1,0:T(1,128)} %bitcast.40, bf16[4,1024]{1,0:T(4,128)(2,1)} %bitcast.38, ...), custom_call_target="tpu_custom_call" | custom-call | flops 603979776 | bytes 4194304 | tf_op jit(solution)/shard_map/level4/pallas_call | solution.py:348
  116.3 11.4 %translate4.1 = bf16[16,2,64,256]{3,2,1,0:T(8,128)(2,1)} custom-call(s32[16,16]{1,0:T(8,128)} %get-tuple-element.20.refs_0_, s32[16,16]{1,0:T(8,128)} %get-tuple-element.21.refs_1_, bf16[1,16,2,64,256]{4,3,2,1,0:T(8,128)(2,1)} %bitcast.32, bf16[316,2,64,256]{3,2,1,0:T(8,128)(2,1)} %refs_3_.4), custom_call_target="tpu_custom_call" | custom-call | flops 33554432 | bytes 22806528 | tf_op jit(solution)/shard_map/translate4/pallas_call | solution.py:443
  (25 shorter events, 0.1 us)
Async XLA Ops:
  4.1 64.0 %copy-start.7 = (bf16[512,4]{0,1:T(4,128)(2,1)S(1)}, bf16[512,4]{0,1:T(4,128)(2,1)}, u32[]{:S(2)}) copy-start(bf16[512,4]{0,1:T(4,128)(2,1)} %param.30) | copy-start | bytes 12292
  4.1 64.0 %copy-start.8 = (s32[512]{0:T(512)S(1)}, s32[512]{0:T(512)}, u32[]{:S(2)}) copy-start(s32[512]{0:T(512)} %param.29) | copy-start | bytes 6148
  4.1 64.0 %copy-start.3 = (s32[128,16]{0,1:T(8,128)S(1)}, s32[128,16]{0,1:T(8,128)}, u32[]{:S(2)}) copy-start(s32[128,16]{0,1:T(8,128)} %param.34) | copy-start | bytes 24580
  4.1 64.0 %copy-start.4 = (s32[128,16]{0,1:T(8,128)S(1)}, s32[128,16]{0,1:T(8,128)}, u32[]{:S(2)}) copy-start(s32[128,16]{0,1:T(8,128)} %param.35) | copy-start | bytes 24580
  4.1 64.6 %copy-start.2 = (f32[512,3]{0,1:T(4,128)S(1)}, f32[512,3]{0,1:T(4,128)}, u32[]{:S(2)}) copy-start(f32[512,3]{0,1:T(4,128)} %constant.44.clone) | copy-start | bytes 18436
  61.6 27.8 %collective-permute-start = (bf16[4,32,2,3,128]{4,3,2,1,0:T(4,128)(2,1)S(1)}, bf16[4,32,2,3,128]{4,3,2,1,0:T(4,128)(2,1)S(1)}, u32[]{:S(2)}, u32[]{:S(2)}) collective-permute-start(bf16[4,32,2,3,128]{4,3,2,1,0:T(4,128)(2,1)S(1)} %get-tuple-element.6), channel_id=1, source_target_pairs={{0,1},{1,2},{2,3},{3,4},{4,5},{5,6},{6,7},{8,9},{9,10},{10,11},{11... | collective-permute-start | bytes 589832 | tf_op jit(solution)/shard_map/ppermute | solution.py:512
  63.8 25.5 %collective-permute-start.1 = (bf16[4,32,2,3,128]{4,3,2,1,0:T(4,128)(2,1)S(1)}, bf16[4,32,2,3,128]{4,3,2,1,0:T(4,128)(2,1)S(1)}, u32[]{:S(2)}, u32[]{:S(2)}) collective-permute-start(bf16[4,32,2,3,128]{4,3,2,1,0:T(4,128)(2,1)S(1)} %get-tuple-element.7), channel_id=1, source_target_pairs={{1,0},{2,1},{3,2},{4,3},{5,4},{6,5},{7,6},{9,8},{10,9},{11,10},{12... | collective-permute-start | bytes 589832 | tf_op jit(solution)/shard_map/ppermute | solution.py:513
  90.8 12.5 %copy-start.5 = (s32[16,16]{1,0:T(8,128)S(1)}, s32[16,16]{1,0:T(8,128)}, u32[]{:S(2)}) copy-start(s32[16,16]{1,0:T(8,128)} %param.37) | copy-start | bytes 3076
  90.8 12.5 %copy-start.6 = (s32[16,16]{1,0:T(8,128)S(1)}, s32[16,16]{1,0:T(8,128)}, u32[]{:S(2)}) copy-start(s32[16,16]{1,0:T(8,128)} %param.38) | copy-start | bytes 3076
  98.2 9.5 %collective-permute-start.2 = (bf16[16,8,512]{2,1,0:T(8,128)(2,1)}, bf16[16,8,512]{2,1,0:T(8,128)(2,1)S(1)}, u32[]{:S(2)}, u32[]{:S(2)}) collective-permute-start(bf16[16,8,512]{2,1,0:T(8,128)(2,1)} %get-tuple-element.5), channel_id=1, source_target_pairs={{0,8},{8,16},{16,24},{24,0},{1,9},{9,17},{17,25},{25,1},{2,10},{10... | collective-permute-start | bytes 393224 | tf_op jit(solution)/shard_map/ppermute | solution.py:541
  101.5 7.4 %collective-permute-start.3 = (bf16[16,8,512]{2,1,0:T(8,128)(2,1)}, bf16[16,8,512]{2,1,0:T(8,128)(2,1)S(1)}, u32[]{:S(2)}, u32[]{:S(2)}) collective-permute-start(bf16[16,8,512]{2,1,0:T(8,128)(2,1)} %get-tuple-element.5), channel_id=1, source_target_pairs={{8,0},{16,8},{24,16},{0,24},{9,1},{17,9},{25,17},{1,25},{10,2},{18... | collective-permute-start | bytes 393224 | tf_op jit(solution)/shard_map/ppermute | solution.py:542
  107.7 1.2 copy-start
  108.9 0.7 copy-start.1

commit v5 on v4

--- a/solution.py
+++ b/solution.py
@@ -537,6 +537,7 @@
         place,
         band_rows,
     )
+    edges4, sources5 = lax.optimization_barrier((edges4, sources5))
     around = [(i, (i + 1) % block_count) for i in range(block_count)]
     from_low = lax.ppermute(edges4, "clu", around)
     from_high = lax.ppermute(edges4, "clu", [(b, a) for a, b in around])

time: 128 us -> 126 us (0.984); the launches traced: 128 us -> 124 us
  waiting for transfers between devices: 5.06 us -> 1.69 us
    ppermute x1, waiting for transfers between devices: 3.87 us -> 0.01 us  [shards(): from_low = lax.ppermute(edges4, 'clu', around)]
where the time goes in v5:
time: 126 us; the launch traced here: 124 us
  Pallas kernels  100 us (79%)
  starting transfers between devices  11.5 us (9%)
  other arithmetic  5.86 us (5%)
  local copies, waits for them, and re-layouts  3.82 us (3%)
  waiting for transfers between devices  1.69 us (1%)
    pallas_call x1, Pallas kernels, produce(): pl.pallas_call(body, grid=(parents,), in_specs=[pl.BlockSpec((8, 8) + chi...  56 us
    pallas_call x2, Pallas kernels, translate(): pl.pallas_call(body, grid_spec=pltpu.PrefetchScalarGridSpec(num_scalar_pr...  30 us
    pallas_call x1, Pallas kernels, halfway(): pl.pallas_call(halfway_kernel, grid_spec=pltpu.PrefetchScalarGridSpec(num...  7.4 us
    pallas_call x1, Pallas kernels, interpolate_phi(): pl.pallas_call(body, grid_spec=pltpu.PrefetchScalarGridSpec(num_scalar_pr...  6.76 us
    ppermute x1, starting transfers between devices, shards(): high = lax.ppermute(arrived5[:, :, :, :3], 'ang', downward)  4.23 us
    ppermute x1, starting transfers between devices, shards(): from_low = lax.ppermute(edges4, 'clu', around)  3.37 us
  transfers between devices with their start and end apart: 4, of which 2 were waited for; matrix products, arithmetic and copies ran while one was open for 2% of the time, Pallas kernels for 15%

profile of v5, /device:TPU:4, one launch (start us, length us, event | category | flops | bytes accessed | tf_op | source)
XLA Modules:
  0.0 123.9 jit_solution(5099770891105609232)
XLA Ops:
  0.6 0.7 fusion.6
  1.4 0.8 copy.35
  2.2 1.0 fusion.2
  3.2 0.8 pad_maximum_fusion
  4.1 56.0 %produce.1 = bf16[128,2,32,128]{3,2,1,0:T(8,128)(2,1)} custom-call(bf16[32,8,2,64,128]{4,3,2,1,0:T(8,128)(2,1)} %bitcast.31, bf16[256,256]{1,0:T(8,128)(2,1)} %bitcast.37, bf16[128,256]{1,0:T(8,128)(2,1)} %refs_2_.1, f32[4,128,256]{2,1,0:T(8,128)} %constant.42.clone.refs_3_, bf16[2,256,512]{2,1,0:T(8,128)(2,1)} %bitcast.34, bf16[256,512]{1,0:T(8,128)(2,1)} %refs_5_.1, ...), custom_call_target="tpu_custom_call" | custom-call | tf_op jit(solution)/shard_map/produce/pallas_call | solution.py:190
  60.2 1.4 %fusion.9 = (bf16[4,32,2,3,128]{4,3,2,1,0:T(4,128)(2,1)S(1)}, bf16[4,32,2,3,128]{4,3,2,1,0:T(4,128)(2,1)S(1)}) fusion(bf16[4,32,2,32,128]{4,3,2,1,0:T(8,128)(2,1)} %bitcast.28), kind=kLoop, calls=%fused_computation.26 | loop fusion | bytes 786432 | tf_op jit(solution)/shard_map/slice | solution.py:512
  61.6 2.2 %collective-permute-start = (bf16[4,32,2,3,128]{4,3,2,1,0:T(4,128)(2,1)S(1)}, bf16[4,32,2,3,128]{4,3,2,1,0:T(4,128)(2,1)S(1)}, u32[]{:S(2)}, u32[]{:S(2)}) collective-permute-start(bf16[4,32,2,3,128]{4,3,2,1,0:T(4,128)(2,1)S(1)} %get-tuple-element.10), channel_id=1, source_target_pairs={{0,1},{1,2},{2,3},{3,4},{4,5},{5,6},{6,7},{8,9},{9,10},{10,11},{11... | collective-permute-start | bytes 589832 | tf_op jit(solution)/shard_map/ppermute | solution.py:512
  63.8 4.2 %collective-permute-start.1 = (bf16[4,32,2,3,128]{4,3,2,1,0:T(4,128)(2,1)S(1)}, bf16[4,32,2,3,128]{4,3,2,1,0:T(4,128)(2,1)S(1)}, u32[]{:S(2)}, u32[]{:S(2)}) collective-permute-start(bf16[4,32,2,3,128]{4,3,2,1,0:T(4,128)(2,1)S(1)} %get-tuple-element.11), channel_id=1, source_target_pairs={{1,0},{2,1},{3,2},{4,3},{5,4},{6,5},{7,6},{9,8},{10,9},{11,10},{12... | collective-permute-start | bytes 589832 | tf_op jit(solution)/shard_map/ppermute | solution.py:513
  68.1 0.8 copy.38.s_ref
  69.0 0.1 pad.2.clone
  69.1 0.6 pad_add_fusion.place.refs_0_
  69.6 0.6 compare_select_fusion
  70.2 1.0 collective-permute-done
  71.3 0.7 collective-permute-done.1
  71.9 1.4 %maximum_maximum_fusion = bf16[4,32,2,16,128]{4,3,2,1,0:T(8,128)(2,1)} fusion(bf16[4,32,2,3,128]{4,3,2,1,0:T(4,128)(2,1)S(1)} %collective-permute-done.1, bf16[4,32,2,3,128]{4,3,2,1,0:T(4,128)(2,1)S(1)} %collective-permute-done, bf16[16]{0:T(256)(128)(2,1)S(1)} %pad.2.clone), kind=kLoop, calls=%fused_computation | loop fusion | flops 3145728 | bytes 1441824 | tf_op jit(solution)/shard_map/concatenate | solution.py:515
  73.4 7.4 %halfway4.1 = (bf16[16,512,128]{2,1,0:T(8,128)(2,1)}, bf16[16,8,512]{2,1,0:T(8,128)(2,1)}) custom-call(s32[2]{0:T(128)} %pad_add_fusion.place.refs_0_, f32[512,8]{1,0:T(8,128)} %copy.38.s_ref, bf16[8,128]{1,0:T(8,128)(2,1)} %constant.45.clone.e_ref, bf16[4,16,2,2,32,128]{5,4,3,2,1,0:T(8,128)(2,1)} %bitcast.29, bf16[4,16,2,2,16,128]{5,4,3,2,1,0:T(8,128)(2,1)} %bitcast.33), custom_call_target="tpu_custom_call" | custom-call | flops 402653184 | bytes 4194304 | tf_op jit(solution)/shard_map/halfway4/pallas_call | solution.py:265
  80.7 3.4 %collective-permute-start.2 = (bf16[16,8,512]{2,1,0:T(8,128)(2,1)}, bf16[16,8,512]{2,1,0:T(8,128)(2,1)S(1)}, u32[]{:S(2)}, u32[]{:S(2)}) collective-permute-start(bf16[16,8,512]{2,1,0:T(8,128)(2,1)} %get-tuple-element.9), channel_id=1, source_target_pairs={{0,8},{8,16},{16,24},{24,0},{1,9},{9,17},{17,25},{25,1},{2,10},{10... | collective-permute-start | bytes 393224 | tf_op jit(solution)/shard_map/ppermute | solution.py:542
  84.1 1.7 %collective-permute-start.3 = (bf16[16,8,512]{2,1,0:T(8,128)(2,1)}, bf16[16,8,512]{2,1,0:T(8,128)(2,1)S(1)}, u32[]{:S(2)}, u32[]{:S(2)}) collective-permute-start(bf16[16,8,512]{2,1,0:T(8,128)(2,1)} %get-tuple-element.9), channel_id=1, source_target_pairs={{8,0},{16,8},{24,16},{0,24},{9,1},{17,9},{25,17},{1,25},{10,2},{18... | collective-permute-start | bytes 393224 | tf_op jit(solution)/shard_map/ppermute | solution.py:543
  85.8 0.6 fusion.8
  86.4 18.7 %translate5.1 = bf16[128,2,32,128]{3,2,1,0:T(8,128)(2,1)} custom-call(s32[16,128]{1,0:T(8,128)} %get-tuple-element.22.refs_0_, s32[16,128]{1,0:T(8,128)} %get-tuple-element.23.refs_1_, bf16[4,32,2,32,128]{4,3,2,1,0:T(8,128)(2,1)} %bitcast.30, bf16[316,2,32,128]{3,2,1,0:T(8,128)(2,1)} %refs_3_.3), custom_call_target="tpu_custom_call" | custom-call | flops 67108864 | bytes 9371648 | tf_op jit(solution)/shard_map/translate5/pallas_call | solution.py:443
  105.2 0.6 copy-done
  105.8 0.0 copy-done.1
  105.9 6.8 %level4.1 = bf16[16,2,64,256]{3,2,1,0:T(8,128)(2,1)} custom-call(s32[2]{0:T(128)} %pad_add_fusion.place.refs_0_, bf16[16,512,128]{2,1,0:T(8,128)(2,1)} %get-tuple-element.8.refs_1_, bf16[16,8,512]{2,1,0:T(8,128)(2,1)} %copy-done, bf16[16,8,512]{2,1,0:T(8,128)(2,1)} %copy-done.1, s32[1,1024]{1,0:T(1,128)} %bitcast.40, bf16[4,1024]{1,0:T(4,128)(2,1)} %bitcast.38, ...), custom_call_target="tpu_custom_call" | custom-call | flops 603979776 | bytes 4194304 | tf_op jit(solution)/shard_map/level4/pallas_call | solution.py:348
  112.6 11.3 %translate4.1 = bf16[16,2,64,256]{3,2,1,0:T(8,128)(2,1)} custom-call(s32[16,16]{1,0:T(8,128)} %get-tuple-element.24.refs_0_, s32[16,16]{1,0:T(8,128)} %get-tuple-element.25.refs_1_, bf16[1,16,2,64,256]{4,3,2,1,0:T(8,128)(2,1)} %bitcast.32, bf16[316,2,64,256]{3,2,1,0:T(8,128)(2,1)} %refs_3_.4), custom_call_target="tpu_custom_call" | custom-call | flops 33554432 | bytes 22806528 | tf_op jit(solution)/shard_map/translate4/pallas_call | solution.py:443
  (25 shorter events, 0.1 us)
Async XLA Ops:
  4.1 64.0 %copy-start.7 = (bf16[512,4]{0,1:T(4,128)(2,1)S(1)}, bf16[512,4]{0,1:T(4,128)(2,1)}, u32[]{:S(2)}) copy-start(bf16[512,4]{0,1:T(4,128)(2,1)} %param.30) | copy-start | bytes 12292
  4.1 64.0 %copy-start.8 = (s32[512]{0:T(512)S(1)}, s32[512]{0:T(512)}, u32[]{:S(2)}) copy-start(s32[512]{0:T(512)} %param.29) | copy-start | bytes 6148
  4.1 64.0 %copy-start.2 = (f32[512,3]{0,1:T(4,128)S(1)}, f32[512,3]{0,1:T(4,128)}, u32[]{:S(2)}) copy-start(f32[512,3]{0,1:T(4,128)} %constant.44.clone) | copy-start | bytes 18436
  4.1 65.5 %copy-start.3 = (s32[16,16]{1,0:T(8,128)S(1)}, s32[16,16]{1,0:T(8,128)}, u32[]{:S(2)}) copy-start(s32[16,16]{1,0:T(8,128)} %param.37) | copy-start | bytes 3076
  4.1 65.5 %copy-start.4 = (s32[16,16]{1,0:T(8,128)S(1)}, s32[16,16]{1,0:T(8,128)}, u32[]{:S(2)}) copy-start(s32[16,16]{1,0:T(8,128)} %param.38) | copy-start | bytes 3076
  61.6 9.7 %collective-permute-start = (bf16[4,32,2,3,128]{4,3,2,1,0:T(4,128)(2,1)S(1)}, bf16[4,32,2,3,128]{4,3,2,1,0:T(4,128)(2,1)S(1)}, u32[]{:S(2)}, u32[]{:S(2)}) collective-permute-start(bf16[4,32,2,3,128]{4,3,2,1,0:T(4,128)(2,1)S(1)} %get-tuple-element.10), channel_id=1, source_target_pairs={{0,1},{1,2},{2,3},{3,4},{4,5},{5,6},{6,7},{8,9},{9,10},{10,11},{11... | collective-permute-start | bytes 589832 | tf_op jit(solution)/shard_map/ppermute | solution.py:512
  63.8 8.1 %collective-permute-start.1 = (bf16[4,32,2,3,128]{4,3,2,1,0:T(4,128)(2,1)S(1)}, bf16[4,32,2,3,128]{4,3,2,1,0:T(4,128)(2,1)S(1)}, u32[]{:S(2)}, u32[]{:S(2)}) collective-permute-start(bf16[4,32,2,3,128]{4,3,2,1,0:T(4,128)(2,1)S(1)} %get-tuple-element.11), channel_id=1, source_target_pairs={{1,0},{2,1},{3,2},{4,3},{5,4},{6,5},{7,6},{9,8},{10,9},{11,10},{12... | collective-permute-start | bytes 589832 | tf_op jit(solution)/shard_map/ppermute | solution.py:513
  73.3 12.5 %copy-start.5 = (s32[128,16]{0,1:T(8,128)S(1)}, s32[128,16]{0,1:T(8,128)}, u32[]{:S(2)}) copy-start(s32[128,16]{0,1:T(8,128)} %param.34) | copy-start | bytes 24580
  73.3 12.5 %copy-start.6 = (s32[128,16]{0,1:T(8,128)S(1)}, s32[128,16]{0,1:T(8,128)}, u32[]{:S(2)}) copy-start(s32[128,16]{0,1:T(8,128)} %param.35) | copy-start | bytes 24580
  80.7 24.4 %collective-permute-start.2 = (bf16[16,8,512]{2,1,0:T(8,128)(2,1)}, bf16[16,8,512]{2,1,0:T(8,128)(2,1)S(1)}, u32[]{:S(2)}, u32[]{:S(2)}) collective-permute-start(bf16[16,8,512]{2,1,0:T(8,128)(2,1)} %get-tuple-element.9), channel_id=1, source_target_pairs={{0,8},{8,16},{16,24},{24,0},{1,9},{9,17},{17,25},{25,1},{2,10},{10... | collective-permute-start | bytes 393224 | tf_op jit(solution)/shard_map/ppermute | solution.py:542
  84.1 21.0 %collective-permute-start.3 = (bf16[16,8,512]{2,1,0:T(8,128)(2,1)}, bf16[16,8,512]{2,1,0:T(8,128)(2,1)S(1)}, u32[]{:S(2)}, u32[]{:S(2)}) collective-permute-start(bf16[16,8,512]{2,1,0:T(8,128)(2,1)} %get-tuple-element.9), channel_id=1, source_target_pairs={{8,0},{16,8},{24,16},{0,24},{9,1},{17,9},{25,17},{1,25},{10,2},{18... | collective-permute-start | bytes 393224 | tf_op jit(solution)/shard_map/ppermute | solution.py:543
  105.2 0.7 copy-start
  105.2 0.7 copy-start.1
